TPU v7x, 32 devices: a whole 2x2x4 slice. The times are simulated.
32 devices in a mesh: wide: 8 (over z, x), blk: 4 (over y, core).
Axes of the slice: x: 2, y: 2, z: 4, core: 2. Of those that a mesh axis runs over, the one named last changes fastest.
Arguments:
- inputs: bfloat16 [16, 512, 768], P('wide', 'blk'), may hold values from -6 to 6
- ln1_gain: float32 [768], replicated, may hold values from 0.5 to 1.5
- ln1_shift: float32 [768], replicated, may hold values from -3 to 3
- w_qkv: bfloat16 [768, 2304], replicated, may hold values from -0.21875 to 0.21875
- q_bias: float32 [768], replicated, may hold values from -3 to 3
- v_bias: float32 [768], replicated, may hold values from -3 to 3
- w_out: bfloat16 [768, 768], replicated, may hold values from -1.25 to 1.25
- out_bias: float32 [768], replicated, may hold values from -3 to 3
- table_x: float32 [64, 12], replicated, may hold values from -3 to 3
- table_y: float32 [64, 12], replicated, may hold values from -3 to 3
- ln2_gain: float32 [768], replicated, may hold values from 0.5 to 1.5
- ln2_shift: float32 [768], replicated, may hold values from -3 to 3
- w_up: bfloat16 [768, 3072], replicated, may hold values from -0.21875 to 0.21875
- up_bias: float32 [3072], replicated, may hold values from -3 to 3
- w_down: bfloat16 [3072, 768], replicated, may hold values from -0.109375 to 0.109375
- down_bias: float32 [768], replicated, may hold values from -3 to 3
- cotangent: bfloat16 [16, 512, 768], P('wide', 'blk'), may hold values from -6 to 6
- page_ids: int32 [16, 512], P('wide'), may hold values from 0 to 4, as said below
- corners: int32 [2, 16, 512], P(None, 'wide'), may hold values from 0 to 768
Outputs:
- output: float32 [16, 512, 768], P('wide', 'blk')
- grad_inputs: float32 [16, 512, 768], P('wide', 'blk')
- grad_ln1_gain: float32 [768], replicated
- grad_ln1_shift: float32 [768], replicated
- grad_w_qkv: float32 [768, 2304], replicated
- grad_q_bias: float32 [768], replicated
- grad_v_bias: float32 [768], replicated
- grad_w_out: float32 [768, 768], replicated
- grad_out_bias: float32 [768], replicated
- grad_table_x: float32 [64, 12], replicated
- grad_table_y: float32 [64, 12], replicated
- grad_ln2_gain: float32 [768], replicated
- grad_ln2_shift: float32 [768], replicated
- grad_w_up: float32 [768, 3072], replicated
- grad_up_bias: float32 [3072], replicated
- grad_w_down: float32 [3072, 768], replicated
- grad_down_bias: float32 [768], replicated
Inputs may be any that keep to these rules, and one draw needn't show every extreme that they name: `page_ids`: along each row page ids start at 0 and never fall, and the row's last position carries page 4; in each row one page covers every position from below 64 to at least 448.
All inputs are finite; a program needn't handle non-finite values.
Results may differ from a plain program's by a relative error of at most 0.012.
Values may be sent and summed in bfloat16 or wider, within the bound.
A program may use at most 192 MiB of HBM per device.

v0:
```python
import math

import jax
import jax.numpy as jnp
from jax import lax
from jax.sharding import PartitionSpec as P

HEADS = 12
HEAD_DIM = 64
BUCKETS = 64
BIN_PX = 16


def layer_stats(values):
    mean_val = jnp.mean(values, axis=-1, keepdims=True)
    centered = values - mean_val
    inv_std = lax.rsqrt(jnp.mean(centered * centered, axis=-1, keepdims=True) + 1e-05)
    return (centered * inv_std, inv_std)


def norm_back(grad_norm, normalized, inv_std, gain):
    scaled = grad_norm * gain
    first_mean = jnp.mean(scaled, axis=-1, keepdims=True)
    second_mean = jnp.mean(scaled * normalized, axis=-1, keepdims=True)
    return inv_std * (scaled - first_mean - normalized * second_mean)


def bin_hot(query_pos, key_pos):
    offset = jnp.floor_divide(key_pos[:, None, :] - query_pos[:, :, None], BIN_PX)
    bins = jnp.clip(offset, -(BUCKETS // 2), BUCKETS // 2 - 1) + BUCKETS // 2
    levels = jnp.arange(BUCKETS, dtype=jnp.int32)[:, None, None, None]
    return (levels == bins[None]).astype(jnp.bfloat16)


def group_scores(heads_q, heads_k, q_x, q_y, q_page, k_x, k_y, k_page, table_x, table_y):
    hot_x = bin_hot(q_x, k_x)
    hot_y = bin_hot(q_y, k_y)
    raw = jnp.einsum(
        "gqhd,gkhd->ghqk", heads_q, heads_k, preferred_element_type=jnp.float32
    ) * HEAD_DIM ** (-0.5)
    bias_x = jnp.einsum(
        "bgqk,bh->ghqk",
        hot_x,
        table_x,
        precision=lax.Precision.HIGHEST,
        preferred_element_type=jnp.float32,
    )
    bias_y = jnp.einsum(
        "bgqk,bh->ghqk",
        hot_y,
        table_y,
        precision=lax.Precision.HIGHEST,
        preferred_element_type=jnp.float32,
    )
    scores = raw + bias_x + bias_y
    same = (q_page[:, :, None] == k_page[:, None, :])[:, None]
    return (jnp.where(same, scores, -1e30), hot_x, hot_y)


def pack_flat(pieces, devices):
    flat = jnp.concatenate([piece.reshape(-1) for piece in pieces])
    extra = -flat.shape[0] % devices
    return flat


def unpack_flat(flat, shapes):
    results = []
    offset = 0
    for shape in shapes:
        length = math.prod(shape)
        results.append(flat[offset : offset + length].reshape(shape))
        offset += length
    return results


def contract_rows(left, right):
    return lax.dot_general(
        left, right, (((0,), (0,)), ((), ())), preferred_element_type=jnp.float32
    )


def contract_cols(left, right):
    return lax.dot_general(
        left, right, (((1,), (1,)), ((), ())), preferred_element_type=jnp.float32
    )


def gelu_exact(values):
    return jax.nn.gelu(values, approximate=False)


def per_device(
    inputs,
    ln1_gain,
    ln1_shift,
    w_qkv,
    q_bias,
    v_bias,
    w_out,
    out_bias,
    table_x,
    table_y,
    ln2_gain,
    ln2_shift,
    w_up,
    up_bias,
    w_down,
    down_bias,
    cotangent,
    page_ids,
    corners,
):
    row_count, local_len, width_dim = inputs.shape
    full_len = page_ids.shape[1]
    token_count = row_count * local_len
    group_rows = min(4, row_count)
    group_count = row_count // group_rows
    devices = lax.axis_size(("wide", "blk"))
    scale = HEAD_DIM ** (-0.5)

    def grouped(array):
        return array.reshape((group_count, group_rows) + array.shape[1:])

    tokens = inputs.reshape(token_count, width_dim).astype(jnp.float32)
    normed_one, inv_one = layer_stats(tokens)
    xn_one = (normed_one * ln1_gain + ln1_shift).astype(jnp.bfloat16)
    joined = jnp.dot(xn_one, w_qkv, preferred_element_type=jnp.float32)
    query = (joined[:, :width_dim] + q_bias).astype(jnp.bfloat16)
    key = joined[:, width_dim : 2 * width_dim].astype(jnp.bfloat16)
    value = (joined[:, 2 * width_dim :] + v_bias).astype(jnp.bfloat16)
    query_rows = query.reshape(row_count, local_len, width_dim)
    key_rows = key.reshape(row_count, local_len, width_dim)
    value_rows = value.reshape(row_count, local_len, width_dim)
    start_pos = lax.axis_index("blk") * local_len
    q_corners = lax.dynamic_slice_in_dim(corners, start_pos, local_len, 2)
    q_pages = lax.dynamic_slice_in_dim(page_ids, start_pos, local_len, 1)
    position_pieces = (
        grouped(q_corners[0]),
        grouped(q_corners[1]),
        grouped(q_pages),
        grouped(corners[0]),
        grouped(corners[1]),
        grouped(page_ids),
    )
    gathered_k, gathered_v = (
        lax.all_gather(key_rows, "blk", axis=1, tiled=True),
        lax.all_gather(value_rows, "blk", axis=1, tiled=True),
    )

    def attend(pieces):
        part_q, part_k, part_v, q_x, q_y, q_page, k_x, k_y, k_page = pieces
        heads_q = part_q.reshape(group_rows, local_len, HEADS, HEAD_DIM)
        heads_k = part_k.reshape(group_rows, full_len, HEADS, HEAD_DIM)
        heads_v = part_v.reshape(group_rows, full_len, HEADS, HEAD_DIM)
        masked, hot_x, hot_y = group_scores(
            heads_q, heads_k, q_x, q_y, q_page, k_x, k_y, k_page, table_x, table_y
        )
        row_max = jnp.max(masked, axis=-1, keepdims=True)
        exp_terms = jnp.exp(masked - row_max)
        row_sum = jnp.sum(exp_terms, axis=-1, keepdims=True)
        weights = (exp_terms / row_sum).astype(jnp.bfloat16)
        mixed = jnp.einsum("ghqk,gkhd->gqhd", weights, heads_v, preferred_element_type=jnp.float32)
        log_sum = (row_max + jnp.log(row_sum))[..., 0]
        return (mixed.reshape(group_rows, local_len, width_dim).astype(jnp.bfloat16), log_sum)

    mixed_all, log_sums = lax.map(
        attend, (grouped(query_rows), grouped(gathered_k), grouped(gathered_v)) + position_pieces
    )
    attended = mixed_all.reshape(token_count, width_dim)
    middle = tokens + (jnp.dot(attended, w_out, preferred_element_type=jnp.float32) + out_bias)
    normed_two, inv_two = layer_stats(middle)
    xn_two = (normed_two * ln2_gain + ln2_shift).astype(jnp.bfloat16)
    hidden = jnp.dot(xn_two, w_up, preferred_element_type=jnp.float32) + up_bias
    active, gelu_pull = jax.vjp(gelu_exact, hidden)
    active_low = active.astype(jnp.bfloat16)
    output = middle + (jnp.dot(active_low, w_down, preferred_element_type=jnp.float32) + down_bias)
    grad_out = cotangent.reshape(token_count, width_dim)
    grad_down_bias = jnp.sum(grad_out, axis=0, dtype=jnp.float32)
    grad_w_down = contract_rows(active_low, grad_out)
    grad_active = contract_cols(grad_out, w_down)
    grad_hidden = gelu_pull(grad_active)[0].astype(jnp.bfloat16)
    grad_up_bias = jnp.sum(grad_hidden, axis=0, dtype=jnp.float32)
    grad_w_up = contract_rows(xn_two, grad_hidden)
    grad_xn_two = contract_cols(grad_hidden, w_up)
    grad_ln2_gain = jnp.sum(grad_xn_two * normed_two, axis=0)
    grad_ln2_shift = jnp.sum(grad_xn_two, axis=0)
    grad_middle = grad_out.astype(jnp.float32) + norm_back(
        grad_xn_two, normed_two, inv_two, ln2_gain
    )
    grad_branch = grad_middle.astype(jnp.bfloat16)
    grad_out_bias = jnp.sum(grad_branch, axis=0, dtype=jnp.float32)
    grad_w_out = contract_rows(attended, grad_branch)
    grad_attended = contract_cols(grad_branch, w_out).astype(jnp.bfloat16)
    back_k, back_v = (gathered_k, gathered_v)

    def attend_back(carry, pieces):
        part_q, part_k, part_v, grad_mix, log_sum, q_x, q_y, q_page, k_x, k_y, k_page = pieces
        heads_q = part_q.reshape(group_rows, local_len, HEADS, HEAD_DIM)
        heads_k = part_k.reshape(group_rows, full_len, HEADS, HEAD_DIM)
        heads_v = part_v.reshape(group_rows, full_len, HEADS, HEAD_DIM)
        grad_heads = grad_mix.reshape(group_rows, local_len, HEADS, HEAD_DIM)
        masked, hot_x, hot_y = group_scores(
            heads_q, heads_k, q_x, q_y, q_page, k_x, k_y, k_page, table_x, table_y
        )
        probs = jnp.exp(masked - log_sum[..., None])
        grad_probs = jnp.einsum(
            "gqhd,gkhd->ghqk", grad_heads, heads_v, preferred_element_type=jnp.float32
        )
        inner = jnp.sum(probs * grad_probs, axis=-1, keepdims=True)
        grad_scores = (probs * (grad_probs - inner)).astype(jnp.bfloat16)
        grad_query = (
            jnp.einsum("ghqk,gkhd->gqhd", grad_scores, heads_k, preferred_element_type=jnp.float32)
            * scale
        ).astype(jnp.bfloat16)
        grad_key = (
            jnp.einsum("ghqk,gqhd->gkhd", grad_scores, heads_q, preferred_element_type=jnp.float32)
            * scale
        )
        grad_value = jnp.einsum(
            "ghqk,gqhd->gkhd",
            probs.astype(jnp.bfloat16),
            grad_heads,
            preferred_element_type=jnp.float32,
        )
        table_gx = carry[0] + jnp.einsum(
            "bgqk,ghqk->bh", hot_x, grad_scores, preferred_element_type=jnp.float32
        )
        table_gy = carry[1] + jnp.einsum(
            "bgqk,ghqk->bh", hot_y, grad_scores, preferred_element_type=jnp.float32
        )
        return (
            (table_gx, table_gy),
            (
                grad_query.reshape(group_rows, local_len, width_dim),
                grad_key.reshape(group_rows, full_len, width_dim),
                grad_value.reshape(group_rows, full_len, width_dim),
            ),
        )

    table_zero = jnp.zeros((BUCKETS, HEADS), jnp.float32)
    tables_grad, back_parts = lax.scan(
        attend_back,
        (table_zero, table_zero),
        (
            grouped(query_rows),
            grouped(back_k),
            grouped(back_v),
            grouped(grad_attended.reshape(row_count, local_len, width_dim)),
            log_sums,
        )
        + position_pieces,
    )
    grad_query_all, grad_key_all, grad_value_all = back_parts
    own_key, own_value = (
        lax.psum_scatter(
            grad_key_all.reshape(row_count, full_len, width_dim),
            "blk",
            scatter_dimension=1,
            tiled=True,
        ),
        lax.psum_scatter(
            grad_value_all.reshape(row_count, full_len, width_dim),
            "blk",
            scatter_dimension=1,
            tiled=True,
        ),
    )
    grad_q_low = grad_query_all.reshape(token_count, width_dim)
    grad_k_low = own_key.reshape(token_count, width_dim).astype(jnp.bfloat16)
    grad_v_low = own_value.reshape(token_count, width_dim).astype(jnp.bfloat16)
    grad_joined = jnp.concatenate((grad_q_low, grad_k_low, grad_v_low), axis=1)
    grad_q_bias = jnp.sum(grad_q_low, axis=0, dtype=jnp.float32)
    grad_v_bias = jnp.sum(grad_v_low, axis=0, dtype=jnp.float32)
    grad_w_qkv = contract_rows(xn_one, grad_joined)
    grad_xn_one = contract_cols(grad_joined, w_qkv)
    grad_ln1_gain = jnp.sum(grad_xn_one * normed_one, axis=0)
    grad_ln1_shift = jnp.sum(grad_xn_one, axis=0)
    grad_inputs = grad_middle + norm_back(grad_xn_one, normed_one, inv_one, ln1_gain)
    small_list = [
        grad_ln1_gain,
        grad_ln1_shift,
        grad_q_bias,
        grad_v_bias,
        grad_out_bias,
        tables_grad[0],
        tables_grad[1],
        grad_ln2_gain,
        grad_ln2_shift,
        grad_up_bias,
        grad_down_bias,
    ]
    small_shapes = [piece.shape for piece in small_list]
    small_flat = pack_flat(small_list, devices)
    summed = (
        lax.psum_scatter(grad_w_qkv.reshape(-1), ("wide", "blk"), scatter_dimension=0, tiled=True),
        lax.psum_scatter(grad_w_out.reshape(-1), ("wide", "blk"), scatter_dimension=0, tiled=True),
        lax.psum_scatter(grad_w_up.reshape(-1), ("wide", "blk"), scatter_dimension=0, tiled=True),
        lax.psum_scatter(grad_w_down.reshape(-1), ("wide", "blk"), scatter_dimension=0, tiled=True),
        lax.psum_scatter(small_flat, ("wide", "blk"), scatter_dimension=0, tiled=True),
    )
    flat_qkv, flat_out, flat_up, flat_down, flat_small = (
        lax.all_gather(summed[0], ("wide", "blk"), axis=0, tiled=True),
        lax.all_gather(summed[1], ("wide", "blk"), axis=0, tiled=True),
        lax.all_gather(summed[2], ("wide", "blk"), axis=0, tiled=True),
        lax.all_gather(summed[3], ("wide", "blk"), axis=0, tiled=True),
        lax.all_gather(summed[4], ("wide", "blk"), axis=0, tiled=True),
    )
    smalls = unpack_flat(flat_small, small_shapes)
    return (
        output.reshape(row_count, local_len, width_dim),
        grad_inputs.reshape(row_count, local_len, width_dim),
        smalls[0],
        smalls[1],
        flat_qkv.reshape(grad_w_qkv.shape),
        smalls[2],
        smalls[3],
        flat_out.reshape(grad_w_out.shape),
        smalls[4],
        smalls[5],
        smalls[6],
        smalls[7],
        smalls[8],
        flat_up.reshape(grad_w_up.shape),
        smalls[9],
        flat_down.reshape(grad_w_down.shape),
        smalls[10],
    )


def solution(mesh):
    placed = (
        P("wide", "blk", None),
        P(),
        P(),
        P(),
        P(),
        P(),
        P(),
        P(),
        P(),
        P(),
        P(),
        P(),
        P(),
        P(),
        P(),
        P(),
        P("wide", "blk", None),
        P("wide", None),
        P(None, "wide", None),
    )
    return jax.shard_map(
        per_device,
        mesh=mesh,
        in_specs=placed,
        out_specs=(
            P("wide", "blk", None),
            P("wide", "blk", None),
            P(),
            P(),
            P(),
            P(),
            P(),
            P(),
            P(),
            P(),
            P(),
            P(),
            P(),
            P(),
            P(),
            P(),
            P(),
        ),
        check_vma=False,
    )
```

profile of v0, /device:TPU:0, one launch (start us, length us, event | category | flops | bytes accessed | tf_op | source)
XLA Modules:
  0.0 976.3 jit_solution(17467646037977331908)
XLA Ops:
  15.1 2.4 fusion.29
  17.6 1.9 copy.73
  19.5 1.9 reshape.310
  21.3 1.6 fusion.34
  23.7 12.9 %fusion.3 = f32[2,128,512,12]{1,3,2,0:T(8,128)} fusion(s32[2,128,512]{1,2,0:T(8,128)S(1)} %get-tuple-element.197, f32[64,12]{0,1:T(8,128)} %param.27), kind=kOutput, calls=%fused_computation.5 | convolution fusion | flops 1216348160 | bytes 6818816 | tf_op jit(solution)/shard_map/while/body/eval_jaxpr/bgqk,bh->ghqk/dot_general | solution.py:41
  36.6 9.1 copy.76
  45.7 12.9 %fusion.1 = f32[2,128,512,12]{1,3,2,0:T(8,128)} fusion(s32[2,128,512]{1,2,0:T(8,128)} %get-tuple-element.198, f32[64,12]{0,1:T(8,128)S(1)} %copy-done.45), kind=kOutput, calls=%fused_computation.2 | convolution fusion | flops 1216348160 | bytes 6818816 | tf_op jit(solution)/shard_map/while/body/eval_jaxpr/bgqk,bh->ghqk/dot_general | solution.py:48
  58.5 9.1 copy.77
  68.4 2.8 copy.74
  71.3 7.1 fusion.67
  78.4 1.6 fusion.9
  81.8 2.6 copy.72
  84.4 5.1 fusion.26
  90.9 1.5 convolution_add_fusion
  92.9 10.4 %convert_reduce_fusion = (f32[3072]{0:T(1024)}, bf16[256,3072]{1,0:T(8,128)(2,1)S(1)}, f32[256,3072]{1,0:T(8,128)}) fusion(f32[256,3072]{1,0:T(8,128)S(1)} %convolution_add_fusion, bf16[256,768]{1,0:T(8,128)(2,1)S(1)} %bitcast.125, bf16[3072,768]{1,0:T(8,128)(2,1)S(1)} %bitcast.140), kind=kOutput, calls=%fused_computation.25 | convolution fusion | flops 1266152448 | bytes 12988416 | tf_op jit(solution)/shard_map/dot_general | solution.py:83
  103.3 2.2 multiply_reduce_fusion.1
  108.6 1.9 copy.79
  110.5 1.9 reshape.315
  112.4 5.9 fusion.12
  118.3 3.6 copy.85
  121.8 10.0 %reduce-scatter.3.cloned.1.call-start = ((), (), s32[]{:S(2)}) async-start(), calls=%async_computation.4 | async-start | bytes 3932160 | tf_op jit(solution)/shard_map/reduce_scatter | solution.py:255
  131.8 6.3 multiply_reduce_fusion
  138.2 3.7 multiply_convert_fusion
  141.9 2.7 convolution_multiply_fusion
  144.6 3.5 copy.83
  148.2 3.1 fusion.48
  151.4 3.2 reshape.324
  154.6 3.8 convert_reduce_fusion.4
  159.7 1.6 convolution_bitcast_fusion
  161.3 6.0 copy.102
  169.0 5.5 fusion.70
  174.5 10.9 %reshape.328 = f32[2359296]{0:T(1024)} reshape(f32[3072,768]{1,0:T(8,128)} %fusion.70) | data formatting | bytes 18874368 | tf_op jit(solution)/shard_map/reshape | solution.py:298
  185.4 1.9 convert_reduce_fusion.3
  187.4 1.9 copy.87
  189.3 13.9 %reduce-scatter.3.cloned.1.call-done = f32[2,128,768]{2,1,0:T(8,128)} async-done(((f32[2,512,768]{2,1,0:T(8,128)}), f32[2,128,768]{2,1,0:T(8,128)}) %reduce-scatter.3.cloned.1.call-update) | async-done | bytes 786448 | tf_op jit(solution)/shard_map/reduce_scatter | solution.py:255
  203.2 1.9 convert_element_type.126
  205.2 1.9 copy.86
  207.0 5.5 fusion.46
  212.5 7.9 reshape.322
  220.5 432.3 %all-reduce.9.cloned.1.call-done = (f32[1769472]{0:T(1024)}, f32[589824]{0:T(1024)}, f32[2359296]{0:T(1024)}, f32[2359296]{0:T(1024)}) async-done(((f32[1769472]{0:T(1024)}, f32[589824]{0:T(1024)}, f32[2359296]{0:T(1024)}, f32[2359296]{0:T(1024)}), (f32[1769472]{0:T(1024)}, f32[589824]{0:T(1024)}, f32[2359296]{0:T(1024)}, f32[2359296]{0:T(1024)})) %all-reduce.9.cloned.1.call-update) | async-done | bytes 28311568
  652.8 1.5 dynamic-slice.6
  654.4 1.6 dynamic-slice.5
  656.1 1.7 dynamic-slice.8
  657.9 1.7 dynamic-slice.7
  660.7 7.8 copy.88
  669.2 7.4 fusion.27
  677.5 7.4 fusion.28
  684.9 1.4 reshape.321
  686.4 5.4 fusion.22
  691.9 2.7 multiply_reduce_fusion.2
  702.4 1.5 constant_dynamic-update-slice_fusion.4
  709.1 41.4 %all-reduce.1 = f32[10752]{0:T(1024)} all-reduce(f32[10752]{0:T(1024)} %constant_dynamic-update-slice_fusion), channel_id=4, replica_groups=mesh['wide'=8,'blk'=4] {'wide','blk'}, use_global_device_ids=true, to_apply=%region_22.23.clone | all-reduce | flops 10752 | bytes 86016
  751.1 1.5 dynamic-slice_dynamic-update-slice_fusion
  752.6 42.1 %all-reduce = f32[10752]{0:T(1024)} all-reduce(f32[10752]{0:T(1024)} %dynamic-slice_dynamic-update-slice_fusion), channel_id=1, replica_groups=mesh['wide'=8,'blk'=4] {'wide','blk'}, use_global_device_ids=true, to_apply=%add | all-reduce | flops 10752 | bytes 86016
  796.0 1.5 fusion.66
  798.1 1.4 copy.93
  800.3 1.4 copy.92
  803.1 2.6 multiply_add_fusion
  805.7 3.4 reshape.325
  809.1 8.2 reshape.323
  817.3 56.6 %all-gather.17.cloned.1.call-done = f32[2359296]{0:T(1024)} async-done(((f32[73728]{0:T(1024)}), f32[2359296]{0:T(1024)}) %all-gather.17.cloned.1.call-update) | async-done | bytes 9437200 | tf_op jit(solution)/shard_map/all_gather | solution.py:305
  873.9 11.3 %reshape.329 = f32[3072,768]{1,0:T(8,128)} reshape(f32[2359296]{0:T(1024)} %all-gather.17.cloned.1.call-done) | data formatting | bytes 18874368 | tf_op jit(solution)/shard_map/reshape | solution.py:325
  885.2 73.3 %all-gather.15.cloned.1.call-done = f32[2359296]{0:T(1024)} async-done(((f32[73728]{0:T(1024)}), f32[2359296]{0:T(1024)}) %all-gather.15.cloned.1.call-update) | async-done | bytes 9437200 | tf_op jit(solution)/shard_map/all_gather | solution.py:304
  958.5 10.9 %reshape.327 = f32[768,3072]{1,0:T(8,128)} reshape(f32[2359296]{0:T(1024)} %all-gather.15.cloned.1.call-done) | data formatting | bytes 18874368 | tf_op jit(solution)/shard_map/reshape | solution.py:323
  (182 shorter events, 39.7 us)
Async XLA Ops:
  7.2 4.4 copy-start
  7.2 61.2 %all-gather.9.cloned.1.call-start = ((), (), s32[]{:S(2)}) async-start(), calls=%async_computation.3 | async-start | bytes 1966080 | tf_op jit(solution)/shard_map/all_gather | solution.py:146
  8.5 1.3 copy-start.41
  11.6 1.1 copy-start.12
  11.6 3.4 copy-start.47
  11.6 3.4 copy-start.48
  12.8 1.4 copy-start.5
  14.2 3.4 copy-start.39
  15.0 66.8 %all-gather.7.cloned.1.call-start = ((), (), s32[]{:S(2)}) async-start(), calls=%async_computation.2 | async-start | bytes 1966080 | tf_op jit(solution)/shard_map/all_gather | solution.py:147
  17.5 167.9 %reduce-scatter.5.cloned.1.call-start = ((), (), s32[]{:S(2)}) async-start(), calls=%async_computation.5 | async-start | bytes 3932160 | tf_op jit(solution)/shard_map/reduce_scatter | solution.py:261
  22.9 0.8 copy-start.14
  36.6 9.1 copy-start.45
  58.5 9.1 copy-start.46
  78.4 2.7 copy-start.1
  78.4 2.7 copy-start.25
  84.4 6.5 slice-start
  84.4 5.5 copy-start.8
  84.4 5.6 copy-start.24
  84.4 5.6 copy-start.52
  84.4 6.5 slice-start.1
  89.5 1.4 copy-start.26
  89.5 1.4 copy-start.28
  89.5 1.4 copy-start.51
  89.9 0.9 copy-start.21
  89.9 2.6 slice-start.2
  90.6 14.9 %copy-start.6 = (f32[256,768]{1,0:T(8,128)}, f32[256,768]{1,0:T(8,128)S(1)}, u32[]{:S(2)}) copy-start(f32[256,768]{1,0:T(8,128)S(1)} %get-tuple-element.190) | copy-start | bytes 2359300
  90.6 14.9 %copy-start.31 = (f32[256]{0:T(256)}, f32[256]{0:T(256)S(1)}, u32[]{:S(2)}) copy-start(f32[256]{0:T(256)S(1)} %broadcast_multiply_fusion.4) | copy-start | bytes 3076
  90.9 14.6 %copy-start.37 = (f32[256]{0:T(256)}, f32[256]{0:T(256)S(1)}, u32[]{:S(2)}) copy-start(f32[256]{0:T(256)S(1)} %add_rsqrt_fusion) | copy-start | bytes 3076
  90.9 1.8 copy-start.10
  90.9 2.0 slice-start.3
  92.4 10.9 %copy-start.15 = (f32[256,3072]{1,0:T(8,128)}, f32[256,3072]{1,0:T(8,128)S(1)}, u32[]{:S(2)}) copy-start(f32[256,3072]{1,0:T(8,128)S(1)} %convolution_add_fusion) | copy-start | bytes 9437188
  103.3 2.2 copy-start.22
  106.4 0.9 copy-start.3
  121.8 81.4 %reduce-scatter.3.cloned.1.call-start = ((), (), s32[]{:S(2)}) async-start(), calls=%async_computation.4 | async-start | bytes 3932160 | tf_op jit(solution)/shard_map/reduce_scatter | solution.py:255
  138.2 3.7 copy-start.13
  141.9 2.7 copy-start.2
  148.2 504.6 %all-reduce.9.cloned.1.call-start = ((), (), s32[]{:S(2)}) async-start(), calls=%async_computation.10 | async-start | bytes 56623104
  154.6 5.0 copy-start.7
  154.6 5.1 copy-start.23
  154.6 5.1 copy-start.27
  154.6 5.1 copy-start.29
  154.6 5.0 copy-start.32
  154.6 5.0 copy-start.38
  161.3 6.0 copy-start.16
  161.3 6.0 copy-start.17
  167.3 1.7 copy-start.11
  167.8 1.1 copy-start.4
  220.4 585.3 %all-gather.13.cloned.1.call-start = ((), (), s32[]{:S(2)}) async-start(), calls=%async_computation.7 | async-start | bytes 2433024 | tf_op jit(solution)/shard_map/all_gather | solution.py:303
  654.3 154.8 %all-gather.11.cloned.1.call-start = ((), (), s32[]{:S(2)}) async-start(), calls=%async_computation.6 | async-start | bytes 7299072 | tf_op jit(solution)/shard_map/all_gather | solution.py:302
  656.0 217.8 %all-gather.17.cloned.1.call-start = ((), (), s32[]{:S(2)}) async-start(), calls=%async_computation.9 | async-start | bytes 9732096 | tf_op jit(solution)/shard_map/all_gather | solution.py:305
  657.8 300.7 %all-gather.15.cloned.1.call-start = ((), (), s32[]{:S(2)}) async-start(), calls=%async_computation.8 | async-start | bytes 9732096 | tf_op jit(solution)/shard_map/all_gather | solution.py:304
  686.3 5.4 copy-start.9
  686.3 5.4 copy-start.18
  686.3 5.4 copy-start.19
  686.3 5.4 copy-start.20
  686.3 5.4 copy-start.33
  686.3 5.4 copy-start.42
  686.4 5.4 copy-start.44
  691.8 5.4 copy-start.36
  691.8 8.0 copy-start.34
  691.8 10.6 %copy-start.35 = (f32[768]{0:T(1024)S(1)}, f32[768]{0:T(1024)}, u32[]{:S(2)}) copy-start(f32[768]{0:T(1024)} %reshape.321) | copy-start | bytes 9220
  691.8 12.1 %copy-start.50 = (f32[768]{0:T(1024)S(1)}, f32[768]{0:T(1024)}, u32[]{:S(2)}) copy-start(f32[768]{0:T(1024)} %get-tuple-element.150) | copy-start | bytes 9220
  691.9 13.3 %copy-start.49 = (f32[768]{0:T(1024)S(1)}, f32[768]{0:T(1024)}, u32[]{:S(2)}) copy-start(f32[768]{0:T(1024)} %get-tuple-element.156) | copy-start | bytes 9220
  691.9 14.6 %copy-start.40 = (f32[3072]{0:T(1024)S(1)}, f32[3072]{0:T(1024)}, u32[]{:S(2)}) copy-start(f32[3072]{0:T(1024)} %get-tuple-element.162) | copy-start | bytes 36868
  (2 other events, 1.2 us)
Sparse Core Ops, SparseCore 0:
  15.1 22.3 all-gather.8
  39.1 19.6 all-gather.6
  122.0 40.6 reduce-scatter.4
  165.2 37.9 reduce-scatter.2
  220.6 432.1 all-reduce.8
  656.0 57.3 all-gather.12
  716.7 72.3 all-gather.10
  793.0 80.8 all-gather.16
  877.8 80.6 all-gather.14
where the time goes:
time: 989 us; the launch traced here: 976 us
  waiting for transfers between devices  576 us (58%)
  local copies, waits for them, and re-layouts  154 us (16%)
  matrix products  112 us (11%)
  blocking collectives  83.5 us (8%)
  other arithmetic  24.4 us (2%)
  between operations  15.1 us (2%)
  starting transfers between devices  10.3 us (1%)
    unnamed x10, waiting for transfers between devices  432 us
    unnamed x2, blocking collectives  83.5 us
    all_gather x1, waiting for transfers between devices, per_device(): lax.all_gather(summed[2], ('wide', 'blk'), axis=0, tiled=True)  73.3 us
    all_gather x1, waiting for transfers between devices, per_device(): lax.all_gather(summed[3], ('wide', 'blk'), axis=0, tiled=True)  56.6 us
    unnamed x134, local copies, waits for them, and re-layouts  38.7 us
  transfers between devices with their start and end apart: 9, of which 4 were waited for; matrix products, arithmetic and copies ran while one was open for 22% of the time, Pallas kernels for 0%

commit v1 on v0

v1 whole, which is shorter than its diff:
```python
import functools
import math

import jax
import jax.numpy as jnp
from jax import lax
from jax.experimental import pallas as pl
from jax.experimental.pallas import tpu as pltpu
from jax.sharding import PartitionSpec as P

HEADS = 12
HEAD_DIM = 64
BUCKETS = 64
BIN_PX = 16
MASKED = -1e30
EPS = 1e-05
MESH = pl.DeviceIdType.MESH
MIB = 1024 * 1024
F32, BF16 = jnp.float32, jnp.bfloat16

BLOCK = 128
OWN = 2 * BLOCK
FULL = 2 * OWN
WIDTH = HEADS * HEAD_DIM
FF = 4 * WIDTH
PAIRS = HEADS // 2

SQUARES = 6
CHUNKS = 2 * SQUARES
SIDE = WIDTH
HALF = SIDE // 2
PIECE = SIDE // 16
SIBLING = ("blk", 1)
ALONG_Y, ALONG_X, NEAR_Z, FAR_Z = ("blk", 2), ("wide", 1), ("wide", 2), ("wide", 4)
STEPS = {"Y": ALONG_Y, "X": ALONG_X, "1": NEAR_Z, "2": FAR_Z}
NAMES = "abcdefghijkl"
ROUTES = ("YX21", "XY12", "YX12", "2YX1", "XY21", "1XY2", "X1Y2", "1YX2", "XY12", "YX12", "YX21", "XY12")
PLAN = (
    ("ab",), ("cd",), ("",), ("",), ("ef",), ("ghab",), ("",), ("",), ("cefdb",), ("",), ("lg",), ("hb",), ("ae",),
    ("gcdb",), ("jifha",), ("kg",),
    ("cesablgdescjafbsdgeichskajdsfckeslhjafdbglkchijg", "ekblihbkjalfiagjdkgliecefchijlkdifdfljhljhikik"),
)
SMALL_ROWS = 24


def outer_steps(wide):
    return tuple(("wide", 1 << level) for level in range(3, wide.bit_length() - 1))


def step_bit(step):
    axis, mask = step
    return lax.rem(lax.div(lax.axis_index(axis), mask), 2)


def step_target(step):
    axis, mask = step
    return {axis: lax.axis_index(axis) + mask * (1 - 2 * step_bit(step))}


def remote(source, target, sems, step):
    return pltpu.make_async_remote_copy(
        source, target, sems.at[0], sems.at[1], device_id=step_target(step), device_id_type=MESH
    )


def greet(steps):
    for step in steps:
        pl.semaphore_signal(
            pltpu.get_barrier_semaphore(), inc=1, device_id=step_target(step), device_id_type=MESH
        )


def lanes(first, size):
    return pl.ds(pl.multiple_of(first, 128), size)


def rows(first, size):
    return pl.ds(pl.multiple_of(first, 16), size)


def dot(left, right):
    return jnp.dot(left, right, preferred_element_type=F32)


def dot_cols(left, right):
    return lax.dot_general(left, right, (((1,), (1,)), ((), ())), preferred_element_type=F32)


def dot_rows(left, right):
    return lax.dot_general(left, right, (((0,), (0,)), ((), ())), preferred_element_type=F32)


def normalize(values):
    mean_val = jnp.mean(values, axis=-1, keepdims=True)
    centered = values - mean_val
    inv_std = lax.rsqrt(jnp.mean(centered * centered, axis=-1, keepdims=True) + EPS)
    return centered * inv_std, inv_std


def norm_back(grad, normed, inv_std, gain):
    scaled = grad * gain
    first_mean = jnp.mean(scaled, axis=-1, keepdims=True)
    second_mean = jnp.mean(scaled * normed, axis=-1, keepdims=True)
    return inv_std * (scaled - first_mean - normed * second_mean)


def add_rows(total, first, inbox, box, count):
    block = min(count, 4 * PIECE)

    def body(i, carry):
        here = rows(first + i * block, block)
        both = total[here, :].astype(F32) + inbox[rows(box + i * block, block), :].astype(F32)
        total[here, :] = both.astype(total.dtype)
        return carry

    lax.fori_loop(0, count // block, body, 0)


def chunk_task(route, outer, mine, inbox, sems, place):
    first, size, box = 0, SIDE, 0
    firsts = []
    free = iter(range(sems.shape[0]))
    for step in route:
        half = size // 2
        bit = step_bit(step)
        keep, give = first + bit * half, first + (1 - bit) * half
        copy = remote(mine.at[rows(give, half), :], inbox.at[pl.ds(box, half), :], sems.at[next(free)], step)
        copy.start()
        yield
        copy.wait()
        add_rows(mine, keep, inbox, box, half)
        firsts.append(first)
        first, size, box = keep, half, box + half
    for step in outer:
        copy = remote(mine.at[rows(first, size), :], inbox.at[pl.ds(box, size), :], sems.at[next(free)], step)
        copy.start()
        copy.wait()
        add_rows(mine, first, inbox, box, size)
        box += size
    kept = pltpu.make_async_copy(mine.at[rows(first, size), :], place(first, size), sems.at[next(free), 0])
    kept.start()
    for step, before in zip(reversed(route), reversed(firsts)):
        source = mine.at[rows(first, size), :] if size == PIECE else place(first, size)
        copy = remote(source, place(first, size), sems.at[next(free)], step)
        copy.start()
        yield
        copy.wait()
        if size == PIECE:
            kept.wait()
        first, size = before, size * 2
    copy = remote(place(0, SIDE), place(0, SIDE), sems.at[next(free)], SIBLING)
    copy.start()
    yield
    copy.wait()


def small_task(steps, total, inbox, sems):
    for slot, step in enumerate(steps):
        copy = remote(total, inbox.at[slot], sems.at[slot], step)
        copy.start()
        yield
        copy.wait()
        total[...] += inbox[slot]


def landing(index, side, o_up, o_down, o_qkv, o_out):
    square, right = divmod(index, 2)
    if square in (0, 2):
        start = side * (2 * SIDE) + square // 2 * SIDE
        return lambda first, size: o_down.at[rows(start + first, size), pl.ds(right * HALF, HALF)]
    if square in (1, 3):
        array, start = o_up, side * (2 * SIDE) + square // 2 * SIDE + right * HALF
    elif index < CHUNKS - 1:
        array, start = o_qkv, side * (3 * HALF) + (index - 8) * HALF
    else:
        array, start = o_out, side * HALF
    return lambda first, size: array.at[rows(first, size), lanes(start, HALF)]


def layer_kernel(
    outer,
    x_in, ln1_gain, ln1_shift, w_qkv_in, q_bias, v_bias, w_out_in, out_bias, table_x, table_y, ln2_gain, ln2_shift,
    w_up_in, up_bias, w_down_in, down_bias, cot_in, page_ids, corners,
    o_output, o_inputs, o_up, o_down, o_qkv, o_out, small,
    w_qkv, w_out, w_up, w_down, mine, inbox, small_in,
    probs, low_a, low_b, low_c, low_d,
    wide_f, key_f, x_all, g_all, xn1, xn2, att, query, keys, values, act, gh, act_give, gh_give,
    gb, gb_all, gatt, gj, gj_all, index_x, index_y, col, one_key, one_query, tables, out_give, out_far, in_give, in_far,
    load_sems, ex_sems, sems, small_sems,
):
    inner = (SIBLING, ALONG_Y, ALONG_X, NEAR_Z, FAR_Z)
    place = lax.axis_index("blk")
    side = step_bit(SIBLING)
    row = step_bit(ALONG_Y)
    other = 1 - row
    blocks = (place, place + 2 - 4 * row, place + 1 - 2 * side, place + 2 - 4 * row + 1 - 2 * side)
    low_lane = lax.broadcasted_iota(jnp.int32, (OWN, 128), 1) < HEAD_DIM
    exchanges = []

    def exchange(source, target, step):
        copy = remote(source, target, ex_sems.at[len(exchanges)], step)
        copy.start()
        exchanges.append(copy)
        return copy

    loads = []
    for slot, (array, held) in enumerate(((w_qkv_in, w_qkv), (w_out_in, w_out), (w_up_in, w_up), (w_down_in, w_down))):
        copy = pltpu.make_async_copy(array, held, load_sems.at[slot])
        copy.start()
        loads.append(copy)

    greet(inner + outer)
    x_all[0:BLOCK, :] = x_in[row]
    g_all[0:BLOCK, :] = cot_in[row]

    tables[0:HEADS, 0:BUCKETS] = table_x[...]
    tables[0:HEADS, BUCKETS : 2 * BUCKETS] = table_y[...]

    def along(kind, block):
        here = lanes(block * BLOCK, BLOCK)
        source = page_ids[:, here] if kind == 2 else corners[kind, :, here]
        return jnp.broadcast_to(jnp.where(row == 0, source[0:1], source[1:2]), (BLOCK, BLOCK))

    for kind in range(3):
        for slot, block in enumerate(blocks):
            down = along(kind, block).astype(F32).T.astype(jnp.int32)
            col[kind, slot * BLOCK : (slot + 1) * BLOCK, :] = down
    lane = lax.broadcasted_iota(jnp.int32, (BLOCK, BLOCK), 1)
    line = lax.broadcasted_iota(jnp.int32, (BLOCK, BLOCK), 0)
    for slot, block in enumerate(blocks):
        part = slice(slot * BLOCK, (slot + 1) * BLOCK)
        bins_x = lax.shift_right_arithmetic(col[0, part, :], 4) + 1
        bins_y = lax.shift_right_arithmetic(col[1, part, :], 4) + 1 + BUCKETS
        one_key[part, :] = jnp.where(lane == jnp.where(lane < BUCKETS, bins_x, bins_y), 1.0, 0.0).astype(BF16)
        if slot < 2:
            turned_x = BUCKETS - 1 - lax.shift_right_arithmetic(along(0, block), 4)
            turned_y = 2 * BUCKETS - 1 - lax.shift_right_arithmetic(along(1, block), 4)
            one_query[:, part] = jnp.where(line == jnp.where(line < BUCKETS, turned_x, turned_y), 1.0, 0.0).astype(BF16)
        for upper in range(2):
            q_part = slice(upper * BLOCK, (upper + 1) * BLOCK)

            def bucket(kind):
                away = lax.shift_right_arithmetic(along(kind, block) - col[kind, q_part, :], 4)
                return jnp.clip(away, -(BUCKETS // 2), BUCKETS // 2 - 1) + BUCKETS // 2

            same = along(2, block) == col[2, q_part, :]
            index_x[q_part, part] = bucket(0)
            index_y[q_part, part] = jnp.where(same, bucket(1) + BUCKETS, -1)

    pl.semaphore_wait(pltpu.get_barrier_semaphore(), len(inner + outer))
    x_copy = exchange(x_in.at[other], x_all.at[pl.ds(BLOCK, BLOCK), :], ALONG_Y)
    g_copy = exchange(cot_in.at[other], g_all.at[pl.ds(BLOCK, BLOCK), :], ALONG_Y)

    def bias_pair(pair, carry):
        for odd in range(2):
            table = tables[pl.ds(2 * pair + odd, 1), :]
            table = jnp.broadcast_to(table, (OWN, 128))
            for slot in range(4):
                part = slice(slot * BLOCK, (slot + 1) * BLOCK)
                at_y = index_y[:, part]
                bias = jnp.take_along_axis(table, index_x[:, part], axis=1, mode="promise_in_bounds") + jnp.take_along_axis(
                    table, jnp.bitwise_and(at_y, 127), axis=1, mode="promise_in_bounds"
                )
                probs[pair, odd * OWN : (odd + 1) * OWN, part] = jnp.where(at_y >= 0, bias, MASKED)
        return carry

    lax.fori_loop(0, 4, bias_pair, 0)

    gain1, shift1 = ln1_gain[...].reshape(1, WIDTH), ln1_shift[...].reshape(1, WIDTH)
    gain2, shift2 = ln2_gain[...].reshape(1, WIDTH), ln2_shift[...].reshape(1, WIDTH)

    def first_norm(part):
        normed, _ = normalize(x_all[part, :].astype(F32))
        xn1[part, :] = (normed * gain1 + shift1).astype(BF16)

    first_norm(slice(0, BLOCK))
    x_copy.wait()
    first_norm(slice(BLOCK, OWN))
    loads[0].wait()
    keys[0:OWN, :] = dot(xn1[0:OWN, :], w_qkv[:, WIDTH : 2 * WIDTH]).astype(BF16)
    k_copy = exchange(keys.at[pl.ds(0, OWN), :], keys.at[pl.ds(OWN, OWN), :], SIBLING)
    values[0:OWN, :] = (dot(xn1[0:OWN, :], w_qkv[:, 2 * WIDTH :]) + v_bias[...].reshape(1, WIDTH)).astype(BF16)
    v_copy = exchange(values.at[pl.ds(0, OWN), :], values.at[pl.ds(OWN, OWN), :], SIBLING)
    xn1_copy = exchange(xn1.at[pl.ds(0, OWN), :], xn1.at[pl.ds(OWN, OWN), :], SIBLING)
    joined = (dot(xn1[0:OWN, :], w_qkv[:, 0:WIDTH]) + q_bias[...].reshape(1, WIDTH)).astype(BF16)
    query[...] = joined * jnp.asarray(HEAD_DIM**-0.5, BF16)
    g_copy.wait()
    gs_copy = exchange(g_all.at[pl.ds(0, OWN), :], g_all.at[pl.ds(OWN, OWN), :], SIBLING)
    lax.fori_loop(4, PAIRS, bias_pair, 0)
    k_copy.wait()
    v_copy.wait()

    def split_heads(two):
        none = jnp.zeros_like(two)
        return jnp.concatenate((jnp.where(low_lane, two, none), jnp.where(low_lane, none, two)), axis=0)

    def join_heads(stacked):
        return jnp.where(low_lane, stacked[0:OWN], stacked[OWN:])

    def attend(pair, carry):
        here = lanes(pair * 128, 128)
        q_two = split_heads(query[:, here])
        for part in quarters:
            masked = dot_cols(q_two[part], keys[:, here]) + probs[pair, part, :]
            terms = jnp.exp(masked - jnp.max(masked, axis=-1, keepdims=True))
            weights = terms * (1.0 / jnp.sum(terms, axis=-1, keepdims=True))
            probs[pair, part, :] = weights
            low_a[part, :] = weights.astype(BF16)
        att[0:OWN, here] = join_heads(dot(low_a[...], values[:, here])).astype(BF16)
        return carry

    quarters = [slice(k * BLOCK, (k + 1) * BLOCK) for k in range(4)]
    lax.fori_loop(0, PAIRS, attend, 0)
    att_copy = exchange(att.at[pl.ds(0, OWN), :], att.at[pl.ds(OWN, OWN), :], SIBLING)
    middle, total, back = wide_f.at[0], wide_f.at[1], wide_f.at[2]
    loads[1].wait()
    total[...] = dot(att[0:OWN, :], w_out[...])

    def second_norm(part):
        here = x_all[part, :].astype(F32) + (total[part, :] + out_bias[...].reshape(1, WIDTH))
        middle[part, :] = here
        normed, _ = normalize(here)
        xn2[part, :] = (normed * gain2 + shift2).astype(BF16)

    for part in quarters[0:2]:
        second_norm(part)
    xn2_copy = exchange(xn2.at[pl.ds(0, OWN), :], xn2.at[pl.ds(OWN, OWN), :], SIBLING)
    loads[2].wait()
    loads[3].wait()

    def feed(number, first, act_to, gh_to):
        for third in range(3):
            here = lanes(first + third * 256, 256)
            there = slice(third * 256, (third + 1) * 256)
            value = dot(xn2[0:OWN, :], w_up[:, here]) + up_bias[here].reshape(1, 256)
            grad = dot_cols(g_all[0:OWN, :], w_down[rows(first + third * 256, 256), :])
            below = 0.5 * (1.0 + lax.erf(value * math.sqrt(0.5)))
            slope = below + value * (jnp.exp(-0.5 * value * value) * (1.0 / math.sqrt(2.0 * math.pi)))
            act_to[:, there] = (value * below).astype(BF16)
            grad_hidden = (grad * slope).astype(BF16)
            gh_to[:, there] = grad_hidden
            small[pl.ds(8 + lax.div(first, WIDTH), 1), there] = jnp.sum(grad_hidden.astype(F32), axis=0, keepdims=True)
        forward = dot(act_to[...], w_down[rows(first, WIDTH), :])
        backward = dot_cols(gh_to[...], w_up[:, lanes(first, WIDTH)])
        if number:
            total[...] += forward
            back[...] += backward
        else:
            total[...] = forward
            back[...] = backward

    def contract(index, first, left, right, width):
        def body(i, carry):
            here = lanes(i * 256, 256)
            mine[index, rows(i * 256, 256), first : first + width] = dot_rows(left[:, here], right[...]).astype(BF16)
            return carry

        lax.fori_loop(0, SIDE // 256, body, 0)

    tasks = {
        name: chunk_task(
            [STEPS[step] for step in ROUTES[k]], outer, mine.at[k // 2, :, pl.ds(k % 2 * HALF, HALF)], inbox.at[k],
            sems.at[k], landing(k, side, o_up, o_down, o_qkv, o_out),
        )
        for k, name in enumerate(NAMES)
    }
    tasks["s"] = small_task(inner + outer, small, small_in, small_sems)
    plan = iter(PLAN)

    def pump():
        for names in next(plan):
            for name in names:
                next(tasks[name], None)

    def feed_half(half):
        given = (1 - side) * (2 * WIDTH) + half * WIDTH
        kept = side * (2 * WIDTH) + half * WIDTH
        feed(2 * half, given, act_give.at[half], gh_give.at[half])
        act_copy = exchange(act_give.at[half], act.at[half, pl.ds(OWN, OWN), :], SIBLING)
        gh_copy = exchange(gh_give.at[half], gh.at[half, pl.ds(OWN, OWN), :], SIBLING)
        if half:
            pump()
        feed(2 * half + 1, kept, act.at[half, pl.ds(0, OWN), :], gh.at[half, pl.ds(0, OWN), :])
        if half:
            pump()
        else:
            gs_copy.wait()
            xn2_copy.wait()
        act_copy.wait()
        contract(2 * half, 0, act.at[half], g_all, WIDTH)
        pump()
        gh_copy.wait()
        contract(2 * half + 1, 0, xn2, gh.at[half], WIDTH)
        pump()

    feed_half(0)
    feed_half(1)

    def second_back(part):
        normed, inv_std = normalize(middle[part, :])
        total[part, :] = middle[part, :] + (total[part, :] + down_bias[...].reshape(1, WIDTH))
        grad = back[part, :]
        grad_out = g_all[part, :].astype(F32)
        grad_middle = grad_out + norm_back(grad, normed, inv_std, gain2)
        middle[part, :] = grad_middle
        low = grad_middle.astype(BF16)
        gb[part, :] = low
        return grad * normed, grad, grad_out, low.astype(F32)

    def sum_up(slots, work):
        for number, part in enumerate(quarters[0:2]):
            for slot, value in zip(slots, work(part)):
                value = jnp.sum(value, axis=0, keepdims=True)
                small[slot : slot + 1, :] = small[slot : slot + 1, :] + value if number else value

    sum_up((5, 6, 7, 4), second_back)
    out_give[...] = total[BLOCK:OWN, :].astype(BF16)
    out_copy = exchange(out_give, out_far, ALONG_Y)
    own_out = pltpu.make_async_copy(total.at[pl.ds(0, BLOCK), :], o_output.at[row], load_sems.at[4])
    own_out.start()
    gb_all[0:OWN, :] = gb[:, lanes(side * 384, 384)]
    gb_copy = exchange(gb.at[:, lanes((1 - side) * 384, 384)], gb_all.at[pl.ds(OWN, OWN), :], SIBLING)
    gatt[...] = dot_cols(gb[...], w_out[...]).astype(BF16)
    pump()

    rest = [jnp.concatenate([along(kind, block)[0:1] for block in blocks], axis=1) for kind in range(2)]
    rest_x, rest_y = (jnp.bitwise_and(value, BIN_PX - 1) for value in rest)

    def attend_back(pair):
        here = slice(pair * 128, pair * 128 + 128)
        q_two, grad_two = split_heads(query[:, here]), split_heads(gatt[:, here])
        for number, part in enumerate(quarters):
            weights = probs[pair, part, :]
            grad_probs = dot_cols(grad_two[part], values[:, here])
            inner_sum = jnp.sum(weights * grad_probs, axis=-1, keepdims=True)
            grad_scores = weights * (grad_probs - inner_sum)
            low_a[part, :] = weights.astype(BF16)
            low_b[part, :] = grad_scores.astype(BF16)
            for kind, key_rest, low in ((0, rest_x, low_c), (1, rest_y, low_d)):
                own_rest = jnp.bitwise_and(col[kind, quarters[number % 2], :], BIN_PX - 1)
                less = key_rest < jnp.concatenate([own_rest] * 4, axis=1)
                low[part, :] = jnp.where(less, grad_scores, 0.0).astype(BF16)
        grad_scores = low_b[...]
        grad_query = join_heads(dot(grad_scores, keys[:, here])) * HEAD_DIM**-0.5
        gj[:, here] = grad_query.astype(BF16)
        grad_key = dot(q_two.T, grad_scores).T
        grad_value = dot(grad_two.T, low_a[...]).T
        total_k, total_v = key_f.at[0], key_f.at[1]
        give_k, give_v = wide_f.at[3], wide_f.at[4]
        total_k[:, here], give_k[:, here] = grad_key[0:OWN], grad_key[OWN:]
        total_v[:, here], give_v[:, here] = grad_value[0:OWN], grad_value[OWN:]
        shared.append(exchange(give_k.at[:, here], key_f.at[2, :, here], SIBLING))
        shared.append(exchange(give_v.at[:, here], key_f.at[3, :, here], SIBLING))

        every = dot(grad_scores, one_key[...])
        both = lax.broadcasted_iota(jnp.int32, (FULL, 128), 1) < BUCKETS
        less = jnp.where(both, dot(low_c[...], one_key[...]), dot(low_d[...], one_key[...]))
        by_key = every - less + pltpu.roll(less, 127, 1)
        upper = by_key.astype(BF16)
        lower = (by_key - upper.astype(F32)).astype(BF16)
        left_half = lax.broadcasted_iota(jnp.int32, (BUCKETS, 128), 1) < BUCKETS
        spot = lax.broadcasted_iota(jnp.int32, (1, 128), 1)
        for odd in range(2):
            mine_part = slice(odd * OWN, (odd + 1) * OWN)
            table = dot(one_query[...], upper[mine_part]) + dot(one_query[...], lower[mine_part])
            found = []
            for part in (table[0:BUCKETS], pltpu.roll(table[BUCKETS:], BUCKETS, 1)):
                skewed = pltpu.roll(jnp.where(left_half, part, 0.0), 0, 1, stride=1, stride_axis=0)
                line_sum = jnp.sum(skewed, axis=0, keepdims=True)
                below = jnp.sum(jnp.where(spot <= 32, line_sum, 0.0), axis=-1, keepdims=True)
                above = jnp.sum(jnp.where(spot >= 95, line_sum, 0.0), axis=-1, keepdims=True)
                inside = pltpu.roll(line_sum, 96, 1)
                found.append(jnp.where(spot == 0, below, jnp.where(spot == BUCKETS - 1, above, inside)))
            merged = jnp.where(spot < BUCKETS, found[0], pltpu.roll(found[1], BUCKETS, 1))
            at = 12 + 2 * pair + odd
            small[at : at + 1, :] = jnp.concatenate((merged, jnp.zeros((1, WIDTH - 128), F32)), axis=1)

    shared = []
    for pair in range(PAIRS):
        attend_back(pair)
        if pair == 0:
            att_copy.wait()
            gb_copy.wait()
            contract(5, HALF, att, gb_all, HALF)
        pump()
    xn1_copy.wait()
    for copy in shared:
        copy.wait()

    def join_kv(part):
        low_k = (key_f[0, part, :] + key_f[2, part, :]).astype(BF16)
        low_v = (key_f[1, part, :] + key_f[3, part, :]).astype(BF16)
        gj[part, WIDTH : 2 * WIDTH] = low_k
        gj[part, 2 * WIDTH :] = low_v
        return gj[part, 0:WIDTH].astype(F32), low_v.astype(F32)

    sum_up((2, 3), join_kv)
    gj_copy = exchange(gj.at[:, lanes((1 - side) * 1152, 1152)], gj_all.at[pl.ds(OWN, OWN), :], SIBLING)
    gj_all[0:OWN, :] = gj[:, lanes(side * 1152, 1152)]
    back[...] = (
        dot_cols(gj[:, 0:WIDTH], w_qkv[:, 0:WIDTH])
        + dot_cols(gj[:, WIDTH : 2 * WIDTH], w_qkv[:, WIDTH : 2 * WIDTH])
        + dot_cols(gj[:, 2 * WIDTH :], w_qkv[:, 2 * WIDTH :])
    )
    gj_copy.wait()
    pump()
    contract(4, 0, xn1, gj_all.at[:, pl.ds(0, WIDTH)], WIDTH)
    pump()
    contract(5, 0, xn1, gj_all.at[:, pl.ds(WIDTH, HALF)], HALF)
    pump()

    def first_back(part):
        normed, inv_std = normalize(x_all[part, :].astype(F32))
        grad = back[part, :]
        middle[part, :] = middle[part, :] + norm_back(grad, normed, inv_std, gain1)
        return grad * normed, grad

    sum_up((0, 1), first_back)
    in_give[...] = middle[BLOCK:OWN, :].astype(BF16)
    in_copy = exchange(in_give, in_far, ALONG_Y)
    own_in = pltpu.make_async_copy(middle.at[pl.ds(0, BLOCK), :], o_inputs.at[row], load_sems.at[5])
    own_in.start()

    pump()
    out_copy.wait()
    own_out.wait()
    in_copy.wait()
    own_in.wait()
    total[0:BLOCK, :] = out_far[...].astype(F32)
    middle[0:BLOCK, :] = in_far[...].astype(F32)
    last = (
        pltpu.make_async_copy(total.at[pl.ds(0, BLOCK), :], o_output.at[other], load_sems.at[4]),
        pltpu.make_async_copy(middle.at[pl.ds(0, BLOCK), :], o_inputs.at[other], load_sems.at[5]),
    )
    for copy in last:
        copy.start()
    for copy in last:
        copy.wait()


def per_device(
    inputs, ln1_gain, ln1_shift, w_qkv, q_bias, v_bias, w_out, out_bias, table_x, table_y, ln2_gain, ln2_shift,
    w_up, up_bias, w_down, down_bias, cotangent, page_ids, corners,
):
    outer = outer_steps(lax.axis_size("wide"))
    slots = 10 + len(outer)
    assert inputs.shape == (2, BLOCK, WIDTH) and lax.axis_size("blk") == 4 and lax.axis_size("wide") >= 8
    hbm = pl.BlockSpec(memory_space=pl.ANY)
    vmem = pl.BlockSpec(memory_space=pltpu.VMEM)
    shape = jax.ShapeDtypeStruct
    args = (
        inputs, ln1_gain, ln1_shift, w_qkv, q_bias, v_bias, w_out, out_bias, table_x.T, table_y.T, ln2_gain, ln2_shift,
        w_up, up_bias, w_down, down_bias, cotangent, page_ids, corners,
    )
    large = (3, 6, 12, 14)
    output, grad_inputs, full_up, full_down, full_qkv, full_out, small = pl.pallas_call(
        functools.partial(layer_kernel, outer),
        out_shape=(
            shape(inputs.shape, F32), shape(inputs.shape, F32),
            shape(w_up.shape, BF16), shape(w_down.shape, BF16), shape(w_qkv.shape, BF16), shape(w_out.shape, BF16),
            shape((SMALL_ROWS, WIDTH), F32),
        ),
        in_specs=[hbm if k in large else vmem for k in range(len(args))],
        out_specs=(hbm,) * 6 + (vmem,),
        scratch_shapes=[
            pltpu.VMEM(w_qkv.shape, BF16), pltpu.VMEM(w_out.shape, BF16),
            pltpu.VMEM(w_up.shape, BF16), pltpu.VMEM(w_down.shape, BF16),
            pltpu.VMEM((SQUARES, SIDE, SIDE), BF16),
            pltpu.VMEM((CHUNKS, SIDE - PIECE + PIECE * len(outer), HALF), BF16),
            pltpu.VMEM((5 + len(outer), SMALL_ROWS, WIDTH), F32),
            pltpu.VMEM((PAIRS, FULL, FULL), F32),
            pltpu.VMEM((FULL, FULL), BF16), pltpu.VMEM((FULL, FULL), BF16),
            pltpu.VMEM((FULL, FULL), BF16), pltpu.VMEM((FULL, FULL), BF16),
            pltpu.VMEM((5, OWN, WIDTH), F32), pltpu.VMEM((4, OWN, WIDTH), F32),
            pltpu.VMEM((OWN, WIDTH), BF16), pltpu.VMEM((FULL, WIDTH), BF16),
            pltpu.VMEM((FULL, WIDTH), BF16), pltpu.VMEM((FULL, WIDTH), BF16), pltpu.VMEM((FULL, WIDTH), BF16),
            pltpu.VMEM((OWN, WIDTH), BF16), pltpu.VMEM((FULL, WIDTH), BF16), pltpu.VMEM((FULL, WIDTH), BF16),
            pltpu.VMEM((2, FULL, WIDTH), BF16), pltpu.VMEM((2, FULL, WIDTH), BF16),
            pltpu.VMEM((2, OWN, WIDTH), BF16), pltpu.VMEM((2, OWN, WIDTH), BF16),
            pltpu.VMEM((OWN, WIDTH), BF16), pltpu.VMEM((FULL, 384), BF16), pltpu.VMEM((OWN, WIDTH), BF16),
            pltpu.VMEM((OWN, 3 * WIDTH), BF16), pltpu.VMEM((FULL, 1152), BF16),
            pltpu.VMEM((OWN, FULL), jnp.int32), pltpu.VMEM((OWN, FULL), jnp.int32),
            pltpu.VMEM((3, FULL, 128), jnp.int32),
            pltpu.VMEM((FULL, 128), BF16), pltpu.VMEM((128, OWN), BF16), pltpu.VMEM((HEADS, 128), F32),
            pltpu.VMEM((BLOCK, WIDTH), BF16), pltpu.VMEM((BLOCK, WIDTH), BF16),
            pltpu.VMEM((BLOCK, WIDTH), BF16), pltpu.VMEM((BLOCK, WIDTH), BF16),
            pltpu.SemaphoreType.DMA((6,)),
            pltpu.SemaphoreType.DMA((32, 2)),
            pltpu.SemaphoreType.DMA((CHUNKS, slots, 2)),
            pltpu.SemaphoreType.DMA((5 + len(outer), 2)),
        ],
        compiler_params=pltpu.CompilerParams(
            collective_id=0, has_side_effects=True, vmem_limit_bytes=63 * MIB
        ),
        cost_estimate=pl.CostEstimate(flops=13 * 10**9, bytes_accessed=3 * 10**7, transcendentals=10**7),
    )(*args)
    ended = finish(full_up, full_down, full_qkv, full_out, output, grad_inputs, small)
    f_up, f_down, f_qkv, f_out, output, grad_inputs, grad_x, grad_y, f_upb = ended[:9]
    f_ln1g, f_ln1s, f_qb, f_vb, f_outb, f_ln2g, f_ln2s, f_downb = ended[9:]
    return (
        output, grad_inputs, f_ln1g, f_ln1s, f_qkv, f_qb, f_vb, f_out, f_outb, grad_x.T, grad_y.T, f_ln2g, f_ln2s,
        f_up, f_upb, f_down, f_downb,
    )


def finish_kernel(*refs):
    small, outs = refs[6], refs[7:]
    for source, target in zip(refs[:6], outs[:6]):
        target[...] = source[...].astype(target.dtype)

    @pl.when(pl.program_id(0) == 0)
    def _():
        outs[6][...] = small[12:SMALL_ROWS, 0:BUCKETS]
        outs[7][...] = small[12:SMALL_ROWS, BUCKETS : 2 * BUCKETS]
        for part in range(FF // WIDTH):
            outs[8][part * WIDTH : (part + 1) * WIDTH] = small[8 + part, :]
        for slot in range(8):
            outs[9 + slot][...] = small[slot, :]


def finish(*arrays):
    steps = 16

    def slab(array):
        if array.ndim == 3:
            return pl.BlockSpec((array.shape[0], array.shape[1] // steps, array.shape[2]), lambda i: (0, i, 0))
        return pl.BlockSpec((array.shape[0] // steps, array.shape[1]), lambda i: (i, 0))

    def whole(shape):
        return pl.BlockSpec(shape, lambda i: (0,) * len(shape))

    little = [(HEADS, BUCKETS)] * 2 + [(FF,)] + [(WIDTH,)] * 8
    slabs = [slab(array) for array in arrays[:6]]
    return pl.pallas_call(
        finish_kernel,
        grid=(steps,),
        out_shape=[jax.ShapeDtypeStruct(array.shape, F32) for array in arrays[:6]]
        + [jax.ShapeDtypeStruct(shape, F32) for shape in little],
        in_specs=slabs + [whole((SMALL_ROWS, WIDTH))],
        out_specs=slabs + [whole(shape) for shape in little],
        compiler_params=pltpu.CompilerParams(vmem_limit_bytes=60 * MIB),
        cost_estimate=pl.CostEstimate(flops=10**7, bytes_accessed=45 * 10**6, transcendentals=0),
    )(*arrays)


def solution(mesh):
    tokens, row_of_blk = P("wide", "blk", None), P("wide", None)
    return jax.shard_map(
        per_device,
        mesh=mesh,
        in_specs=(tokens,) + (P(),) * 15 + (tokens, row_of_blk, P(None, "wide", None)),
        out_specs=(tokens, tokens) + (P(),) * 15,
        check_vma=False,
    )
```

time: 989 us -> 177 us (0.18); the launches traced: 976 us -> 177 us
  waiting for transfers between devices: 576 us -> 0 us
  Pallas kernels: 0 us -> 176 us
  local copies, waits for them, and re-layouts: 154 us -> 0 us
  matrix products: 112 us -> 0 us
  blocking collectives: 83.5 us -> 0 us
  other arithmetic: 24.4 us -> 0 us
  between operations: 15.1 us -> 0.85 us
  starting transfers between devices: 10.3 us -> 0 us
    unnamed x10 -> x0, waiting for transfers between devices: 432 us -> none
    pallas_call x0 -> x2, Pallas kernels: none -> 176 us  [the longest x1 158 us: per_device(): pl.pallas_call(functools.partial(layer_kernel, outer), out_shape=(shape(i...]
    all_gather x6 -> x0, waiting for transfers between devices: 130 us -> none  [the longest x1 73.3 us: per_device(): lax.all_gather(summed[2], ('wide', 'blk'), axis=0, tiled=True)]
    dot_general x22 -> x0, matrix products: 112 us -> none  [the longest x4 16.5 us: contract_cols(): lax.dot_general(left, right, (((1,), (1,)), ((), ())), preferred_element_...]
    unnamed x2 -> x0, blocking collectives: 83.5 us -> none
    reshape x13 -> x0, local copies, waits for them, and re-layouts: 68.9 us -> none  [the longest x1 11.3 us: per_device(): flat_down.reshape(grad_w_down.shape)]
    unnamed x134 -> x0, local copies, waits for them, and re-layouts: 38.7 us -> none
    dot_general x2 -> x0, local copies, waits for them, and re-layouts: 18.2 us -> none  [the longest x1 9.08 us: group_scores(): jnp.einsum('bgqk,bh->ghqk', hot_x, table_x, precision=lax.Precision.HIGHE...]
  transfers between devices with their start and end apart: 9 -> 0, of which waited for: 4 -> 0; matrix products, arithmetic and copies ran while one was open for 22% -> 0% of each run, Pallas kernels for 0% -> 0%
where the time goes in v1:
time: 177 us
  Pallas kernels  176 us (99%)
    pallas_call x1, Pallas kernels, per_device(): pl.pallas_call(functools.partial(layer_kernel, outer), out_shape=(shape(i...  158 us
    pallas_call x1, Pallas kernels, finish(): pl.pallas_call(finish_kernel, grid=(steps,), out_shape=[jax.ShapeDtypeStr...  17.6 us

profile of v1, /device:TPU:0, one launch (start us, length us, event | category | flops | bytes accessed | tf_op | source)
XLA Modules:
  0.0 176.8 jit_solution(11556331734991049576)
XLA Ops:
  0.7 158.3 %shard_map.314 = (f32[2,128,768]{2,1,0:T(8,128)}, f32[2,128,768]{2,1,0:T(8,128)}, bf16[768,3072]{1,0:T(8,128)(2,1)}, bf16[3072,768]{1,0:T(8,128)(2,1)}, bf16[768...) custom-call(bf16[2,128,768]{2,1,0:T(8,128)(2,1)} %x_in.1, f32[768]{0:T(1024)} %ln1_gain.1, ...), custom_call_target="tpu_custom_call" | custom-call | flops 12999999488 | bytes 30000000 | tf_op jit(solution)/shard_map/pallas_call | solution.py:556
  159.0 17.6 %shard_map.315 = (f32[768,3072]{1,0:T(8,128)}, f32[3072,768]{1,0:T(8,128)}, f32[768,2304]{1,0:T(8,128)}, f32[768,768]{1,0:T(8,128)}, f32[2,128,768]{2,1,0:T(8,12...) custom-call(bf16[768,3072]{1,0:T(8,128)(2,1)} %get-tuple-element.41., ...), custom_call_target="tpu_custom_call" | custom-call | flops 10000000 | bytes 45000000 | tf_op jit(solution)/shard_map/pallas_call | solution.py:634

commit v2 on v1

--- a/solution.py
+++ b/solution.py
@@ -34,13 +34,16 @@
 ALONG_Y, ALONG_X, NEAR_Z, FAR_Z = ("blk", 2), ("wide", 1), ("wide", 2), ("wide", 4)
 STEPS = {"Y": ALONG_Y, "X": ALONG_X, "1": NEAR_Z, "2": FAR_Z}
 NAMES = "abcdefghijkl"
-ROUTES = ("YX21", "XY12", "YX12", "2YX1", "XY21", "1XY2", "X1Y2", "1YX2", "XY12", "YX12", "YX21", "XY12")
+ROUTES = ("XY21", "YX12", "1X2Y", "YX12", "XY12", "YX12", "YX12", "1YX2", "XY12", "XY21", "YX12", "12YX")
 PLAN = (
-    ("ab",), ("cd",), ("",), ("",), ("ef",), ("ghab",), ("",), ("",), ("cefdb",), ("",), ("lg",), ("hb",), ("ae",),
-    ("gcdb",), ("jifha",), ("kg",),
-    ("cesablgdescjafbsdgeichskajdsfckeslhjafdbglkchijg", "ekblihbkjalfiagjdkgliecefchijlkdifdfljhljhikik"),
+    ("ab",), ("cd",), ("",), ("",), ("ef",), ("h",), ("abc",), ("lde",), ("hb",), ("fc",), ("gld",), ("b",),
+    ("fac",), ("ed",), ("ijhl",), ("kbf",),
+    ("segacsdlbifaedbkajfhedcgsflaheibgjckhiadgsekjfil", "gsjcbkhigbjsdadacfkicelfkejghikljhhigilgljkjk"),
 )
 SMALL_ROWS = 24
+
+SLAB = 384 * WIDTH
+SLOTS = 8
 
 
 def outer_steps(wide):
@@ -179,13 +182,15 @@
 
 def layer_kernel(
     outer,
-    x_in, ln1_gain, ln1_shift, w_qkv_in, q_bias, v_bias, w_out_in, out_bias, table_x, table_y, ln2_gain, ln2_shift,
-    w_up_in, up_bias, w_down_in, down_bias, cot_in, page_ids, corners,
-    o_output, o_inputs, o_up, o_down, o_qkv, o_out, small,
+    x_in, ln1_gain_in, ln1_shift_in, w_qkv_in, q_bias_in, v_bias_in, w_out_in, out_bias_in, table_x_in, table_y_in,
+    ln2_gain_in, ln2_shift_in, w_up_in, up_bias_in, w_down_in, down_bias_in, cot_in, page_ids_in, corners_in,
+    o_output, o_inputs, o_up, o_down, o_qkv, o_out, o_small,
+    ln1_gain, ln1_shift, q_bias, v_bias, out_bias, ln2_gain, ln2_shift, down_bias, up_bias, table_x, table_y,
+    page_ids, corners, small,
     w_qkv, w_out, w_up, w_down, mine, inbox, small_in,
     probs, low_a, low_b, low_c, low_d,
     wide_f, key_f, x_all, g_all, xn1, xn2, att, query, keys, values, act, gh, act_give, gh_give,
-    gb, gb_all, gatt, gj, gj_all, index_x, index_y, col, one_key, one_query, tables, out_give, out_far, in_give, in_far,
+    gb, gb_all, gatt, gj, gj_all, col, key_twice, one_key, one_query, tables, out_give, out_far, in_give, in_far,
     load_sems, ex_sems, sems, small_sems,
 ):
     inner = (SIBLING, ALONG_Y, ALONG_X, NEAR_Z, FAR_Z)
@@ -203,18 +208,29 @@
         exchanges.append(copy)
         return copy
 
-    loads = []
-    for slot, (array, held) in enumerate(((w_qkv_in, w_qkv), (w_out_in, w_out), (w_up_in, w_up), (w_down_in, w_down))):
-        copy = pltpu.make_async_copy(array, held, load_sems.at[slot])
-        copy.start()
-        loads.append(copy)
-
     greet(inner + outer)
-    x_all[0:BLOCK, :] = x_in[row]
-    g_all[0:BLOCK, :] = cot_in[row]
-
-    tables[0:HEADS, 0:BUCKETS] = table_x[...]
-    tables[0:HEADS, BUCKETS : 2 * BUCKETS] = table_y[...]
+    pairs = (
+        (corners_in, corners), (page_ids_in, page_ids), (table_x_in, table_x), (table_y_in, table_y),
+        (x_in.at[row], x_all.at[pl.ds(0, BLOCK), :]),
+        (ln1_gain_in, ln1_gain), (ln1_shift_in, ln1_shift), (v_bias_in, v_bias),
+        (w_qkv_in, w_qkv),
+        (q_bias_in, q_bias), (cot_in.at[row], g_all.at[pl.ds(0, BLOCK), :]), (out_bias_in, out_bias),
+        (ln2_gain_in, ln2_gain), (ln2_shift_in, ln2_shift), (down_bias_in, down_bias), (up_bias_in, up_bias),
+        (w_out_in, w_out), (w_up_in, w_up), (w_down_in, w_down),
+    )
+    loads = [pltpu.make_async_copy(source, held, load_sems.at[k]) for k, (source, held) in enumerate(pairs)]
+    waited = iter(loads)
+
+    def loaded(count):
+        for _ in range(count):
+            next(waited).wait()
+
+    for copy in loads:
+        copy.start()
+    pl.semaphore_wait(pltpu.get_barrier_semaphore(), len(inner + outer))
+    x_copy = exchange(x_in.at[other], x_all.at[pl.ds(BLOCK, BLOCK), :], ALONG_Y)
+    g_copy = exchange(cot_in.at[other], g_all.at[pl.ds(BLOCK, BLOCK), :], ALONG_Y)
+    loaded(4)
 
     def along(kind, block):
         here = lanes(block * BLOCK, BLOCK)
@@ -236,59 +252,77 @@
             turned_x = BUCKETS - 1 - lax.shift_right_arithmetic(along(0, block), 4)
             turned_y = 2 * BUCKETS - 1 - lax.shift_right_arithmetic(along(1, block), 4)
             one_query[:, part] = jnp.where(line == jnp.where(line < BUCKETS, turned_x, turned_y), 1.0, 0.0).astype(BF16)
-        for upper in range(2):
-            q_part = slice(upper * BLOCK, (upper + 1) * BLOCK)
-
-            def bucket(kind):
-                away = lax.shift_right_arithmetic(along(kind, block) - col[kind, q_part, :], 4)
-                return jnp.clip(away, -(BUCKETS // 2), BUCKETS // 2 - 1) + BUCKETS // 2
-
-            same = along(2, block) == col[2, q_part, :]
-            index_x[q_part, part] = bucket(0)
-            index_y[q_part, part] = jnp.where(same, bucket(1) + BUCKETS, -1)
-
-    pl.semaphore_wait(pltpu.get_barrier_semaphore(), len(inner + outer))
-    x_copy = exchange(x_in.at[other], x_all.at[pl.ds(BLOCK, BLOCK), :], ALONG_Y)
-    g_copy = exchange(cot_in.at[other], g_all.at[pl.ds(BLOCK, BLOCK), :], ALONG_Y)
+    key_rows = [jnp.concatenate([along(kind, block)[0:1] for block in blocks], axis=1) for kind in range(3)]
+    rest_x, rest_y = (jnp.bitwise_and(key_rows[kind], BIN_PX - 1) for kind in range(2))
+
+    def own_lanes(kind, part, mask):
+        return jnp.concatenate([jnp.bitwise_and(col[kind, part, :], mask)] * 4, axis=1)
+
+
+    at = lax.broadcasted_iota(jnp.int32, (16, 128), 1)
+    at = jnp.where(at < BUCKETS, jnp.minimum(at, BUCKETS // 2 - 1), jnp.maximum(at - 128, -(BUCKETS // 2))) + BUCKETS // 2
+    for kind, table in enumerate((table_x, table_y)):
+        tables[0, 0:HEADS, kind * BUCKETS : (kind + 1) * BUCKETS] = table[...]
+    for kind in range(2):
+        distance = jnp.take_along_axis(tables[0], at + kind * BUCKETS, axis=1, mode="promise_in_bounds")
+        for slot, value in ((1, distance), (3, pltpu.roll(distance, 1, 1) - distance)):
+            upper = value.astype(BF16).astype(F32)
+            tables[kind * 4 + slot] = upper
+            tables[kind * 4 + slot + 1] = value - upper
+
+    square_lane = lax.broadcasted_iota(jnp.int32, (128, 128), 1) < BUCKETS
+    square_line = lax.broadcasted_iota(jnp.int32, (128, 128), 0) < BUCKETS
+    diagonal = square_lane == square_line
+    lane_x = jnp.bitwise_and(lax.broadcasted_iota(jnp.int32, (OWN, 256), 1), 127) < BUCKETS
+    key_twice[...] = jnp.concatenate((one_key[...], one_key[...]), axis=1)
 
     def bias_pair(pair, carry):
         for odd in range(2):
-            table = tables[pl.ds(2 * pair + odd, 1), :]
-            table = jnp.broadcast_to(table, (OWN, 128))
-            for slot in range(4):
-                part = slice(slot * BLOCK, (slot + 1) * BLOCK)
-                at_y = index_y[:, part]
-                bias = jnp.take_along_axis(table, index_x[:, part], axis=1, mode="promise_in_bounds") + jnp.take_along_axis(
-                    table, jnp.bitwise_and(at_y, 127), axis=1, mode="promise_in_bounds"
-                )
-                probs[pair, odd * OWN : (odd + 1) * OWN, part] = jnp.where(at_y >= 0, bias, MASKED)
+            squares = []
+            for slot in range(1, 5):
+                both = [jnp.broadcast_to(tables[kind * 4 + slot, pl.ds(2 * pair + odd, 1), :], (BUCKETS, 128)) for kind in range(2)]
+                moved = pltpu.roll(jnp.concatenate(both, axis=0), 0, 1, stride=1, stride_axis=0)
+                squares.append(jnp.where(diagonal, moved, 0.0).astype(BF16))
+            picked = dot(one_key[0:OWN, :], jnp.concatenate(squares, axis=1))
+            plain, change = picked[:, 0:256].astype(BF16), picked[:, 256:512]
+            change_x = jnp.where(lane_x, change, 0.0).astype(BF16)
+            change_y = jnp.where(lane_x, 0.0, change).astype(BF16)
+            terms = dot_cols(jnp.concatenate((plain, change_x, change_y), axis=0), key_twice[...])
+            for number in range(2):
+                part = quarters[number]
+                bias = terms[part]
+                bias += jnp.where(rest_x < own_lanes(0, part, BIN_PX - 1), terms[OWN : 2 * OWN][part], 0.0)
+                bias += jnp.where(rest_y < own_lanes(1, part, BIN_PX - 1), terms[2 * OWN :][part], 0.0)
+                same = key_rows[2] == own_lanes(2, part, 7)
+                probs[pair, odd * OWN + number * BLOCK : odd * OWN + (number + 1) * BLOCK, :] = jnp.where(same, bias, MASKED)
         return carry
 
-    lax.fori_loop(0, 4, bias_pair, 0)
-
+    quarters = [slice(k * BLOCK, (k + 1) * BLOCK) for k in range(4)]
+    loaded(5)
     gain1, shift1 = ln1_gain[...].reshape(1, WIDTH), ln1_shift[...].reshape(1, WIDTH)
-    gain2, shift2 = ln2_gain[...].reshape(1, WIDTH), ln2_shift[...].reshape(1, WIDTH)
+    shared = []
 
     def first_norm(part):
         normed, _ = normalize(x_all[part, :].astype(F32))
         xn1[part, :] = (normed * gain1 + shift1).astype(BF16)
-
-    first_norm(slice(0, BLOCK))
+        keys[part, :] = dot(xn1[part, :], w_qkv[:, WIDTH : 2 * WIDTH]).astype(BF16)
+        values[part, :] = (dot(xn1[part, :], w_qkv[:, 2 * WIDTH :]) + v_bias[...].reshape(1, WIDTH)).astype(BF16)
+        for held in (keys, values):
+            shared.append(exchange(held.at[part, :], held.at[pl.ds(OWN + part.start, BLOCK), :], SIBLING))
+
+    first_norm(quarters[0])
+    lax.fori_loop(0, 4, bias_pair, 0)
+
+    loaded(8)
+    gain2, shift2 = ln2_gain[...].reshape(1, WIDTH), ln2_shift[...].reshape(1, WIDTH)
     x_copy.wait()
-    first_norm(slice(BLOCK, OWN))
-    loads[0].wait()
-    keys[0:OWN, :] = dot(xn1[0:OWN, :], w_qkv[:, WIDTH : 2 * WIDTH]).astype(BF16)
-    k_copy = exchange(keys.at[pl.ds(0, OWN), :], keys.at[pl.ds(OWN, OWN), :], SIBLING)
-    values[0:OWN, :] = (dot(xn1[0:OWN, :], w_qkv[:, 2 * WIDTH :]) + v_bias[...].reshape(1, WIDTH)).astype(BF16)
-    v_copy = exchange(values.at[pl.ds(0, OWN), :], values.at[pl.ds(OWN, OWN), :], SIBLING)
+    first_norm(quarters[1])
     xn1_copy = exchange(xn1.at[pl.ds(0, OWN), :], xn1.at[pl.ds(OWN, OWN), :], SIBLING)
     joined = (dot(xn1[0:OWN, :], w_qkv[:, 0:WIDTH]) + q_bias[...].reshape(1, WIDTH)).astype(BF16)
     query[...] = joined * jnp.asarray(HEAD_DIM**-0.5, BF16)
-    g_copy.wait()
-    gs_copy = exchange(g_all.at[pl.ds(0, OWN), :], g_all.at[pl.ds(OWN, OWN), :], SIBLING)
     lax.fori_loop(4, PAIRS, bias_pair, 0)
-    k_copy.wait()
-    v_copy.wait()
+    for copy in shared:
+        copy.wait()
 
     def split_heads(two):
         none = jnp.zeros_like(two)
@@ -309,11 +343,11 @@
         att[0:OWN, here] = join_heads(dot(low_a[...], values[:, here])).astype(BF16)
         return carry
 
-    quarters = [slice(k * BLOCK, (k + 1) * BLOCK) for k in range(4)]
     lax.fori_loop(0, PAIRS, attend, 0)
     att_copy = exchange(att.at[pl.ds(0, OWN), :], att.at[pl.ds(OWN, OWN), :], SIBLING)
+    g_copy.wait()
+    gs_copy = exchange(g_all.at[pl.ds(0, OWN), :], g_all.at[pl.ds(OWN, OWN), :], SIBLING)
     middle, total, back = wide_f.at[0], wide_f.at[1], wide_f.at[2]
-    loads[1].wait()
     total[...] = dot(att[0:OWN, :], w_out[...])
 
     def second_norm(part):
@@ -325,10 +359,9 @@
     for part in quarters[0:2]:
         second_norm(part)
     xn2_copy = exchange(xn2.at[pl.ds(0, OWN), :], xn2.at[pl.ds(OWN, OWN), :], SIBLING)
-    loads[2].wait()
-    loads[3].wait()
-
-    def feed(number, first, act_to, gh_to):
+    loaded(2)
+
+    def feed(first, act_to, gh_to):
         for third in range(3):
             here = lanes(first + third * 256, 256)
             there = slice(third * 256, (third + 1) * 256)
@@ -340,8 +373,10 @@
             grad_hidden = (grad * slope).astype(BF16)
             gh_to[:, there] = grad_hidden
             small[pl.ds(8 + lax.div(first, WIDTH), 1), there] = jnp.sum(grad_hidden.astype(F32), axis=0, keepdims=True)
-        forward = dot(act_to[...], w_down[rows(first, WIDTH), :])
-        backward = dot_cols(gh_to[...], w_up[:, lanes(first, WIDTH)])
+
+    def gather(number, first, act_from, gh_from):
+        forward = dot(act_from[...], w_down[rows(first, WIDTH), :])
+        backward = dot_cols(gh_from[...], w_up[:, lanes(first, WIDTH)])
         if number:
             total[...] += forward
             back[...] += backward
@@ -375,12 +410,13 @@
     def feed_half(half):
         given = (1 - side) * (2 * WIDTH) + half * WIDTH
         kept = side * (2 * WIDTH) + half * WIDTH
-        feed(2 * half, given, act_give.at[half], gh_give.at[half])
+        own_act, own_gh = act.at[half, pl.ds(0, OWN), :], gh.at[half, pl.ds(0, OWN), :]
+        feed(given, act_give.at[half], gh_give.at[half])
         act_copy = exchange(act_give.at[half], act.at[half, pl.ds(OWN, OWN), :], SIBLING)
         gh_copy = exchange(gh_give.at[half], gh.at[half, pl.ds(OWN, OWN), :], SIBLING)
         if half:
             pump()
-        feed(2 * half + 1, kept, act.at[half, pl.ds(0, OWN), :], gh.at[half, pl.ds(0, OWN), :])
+        feed(kept, own_act, own_gh)
         if half:
             pump()
         else:
@@ -392,6 +428,8 @@
         gh_copy.wait()
         contract(2 * half + 1, 0, xn2, gh.at[half], WIDTH)
         pump()
+        gather(2 * half, given, act_give.at[half], gh_give.at[half])
+        gather(2 * half + 1, kept, own_act, own_gh)
 
     feed_half(0)
     feed_half(1)
@@ -416,15 +454,12 @@
     sum_up((5, 6, 7, 4), second_back)
     out_give[...] = total[BLOCK:OWN, :].astype(BF16)
     out_copy = exchange(out_give, out_far, ALONG_Y)
-    own_out = pltpu.make_async_copy(total.at[pl.ds(0, BLOCK), :], o_output.at[row], load_sems.at[4])
+    own_out = pltpu.make_async_copy(total.at[pl.ds(0, BLOCK), :], o_output.at[row], load_sems.at[19])
     own_out.start()
     gb_all[0:OWN, :] = gb[:, lanes(side * 384, 384)]
     gb_copy = exchange(gb.at[:, lanes((1 - side) * 384, 384)], gb_all.at[pl.ds(OWN, OWN), :], SIBLING)
     gatt[...] = dot_cols(gb[...], w_out[...]).astype(BF16)
     pump()
-
-    rest = [jnp.concatenate([along(kind, block)[0:1] for block in blocks], axis=1) for kind in range(2)]
-    rest_x, rest_y = (jnp.bitwise_and(value, BIN_PX - 1) for value in rest)
 
     def attend_back(pair):
         here = slice(pair * 128, pair * 128 + 128)
@@ -437,8 +472,7 @@
             low_a[part, :] = weights.astype(BF16)
             low_b[part, :] = grad_scores.astype(BF16)
             for kind, key_rest, low in ((0, rest_x, low_c), (1, rest_y, low_d)):
-                own_rest = jnp.bitwise_and(col[kind, quarters[number % 2], :], BIN_PX - 1)
-                less = key_rest < jnp.concatenate([own_rest] * 4, axis=1)
+                less = key_rest < own_lanes(kind, quarters[number % 2], BIN_PX - 1)
                 low[part, :] = jnp.where(less, grad_scores, 0.0).astype(BF16)
         grad_scores = low_b[...]
         grad_query = join_heads(dot(grad_scores, keys[:, here])) * HEAD_DIM**-0.5
@@ -518,7 +552,7 @@
     sum_up((0, 1), first_back)
     in_give[...] = middle[BLOCK:OWN, :].astype(BF16)
     in_copy = exchange(in_give, in_far, ALONG_Y)
-    own_in = pltpu.make_async_copy(middle.at[pl.ds(0, BLOCK), :], o_inputs.at[row], load_sems.at[5])
+    own_in = pltpu.make_async_copy(middle.at[pl.ds(0, BLOCK), :], o_inputs.at[row], load_sems.at[20])
     own_in.start()
 
     pump()
@@ -529,8 +563,9 @@
     total[0:BLOCK, :] = out_far[...].astype(F32)
     middle[0:BLOCK, :] = in_far[...].astype(F32)
     last = (
-        pltpu.make_async_copy(total.at[pl.ds(0, BLOCK), :], o_output.at[other], load_sems.at[4]),
-        pltpu.make_async_copy(middle.at[pl.ds(0, BLOCK), :], o_inputs.at[other], load_sems.at[5]),
+        pltpu.make_async_copy(total.at[pl.ds(0, BLOCK), :], o_output.at[other], load_sems.at[19]),
+        pltpu.make_async_copy(middle.at[pl.ds(0, BLOCK), :], o_inputs.at[other], load_sems.at[20]),
+        pltpu.make_async_copy(small, o_small, load_sems.at[21]),
     )
     for copy in last:
         copy.start()
@@ -546,13 +581,11 @@
     slots = 10 + len(outer)
     assert inputs.shape == (2, BLOCK, WIDTH) and lax.axis_size("blk") == 4 and lax.axis_size("wide") >= 8
     hbm = pl.BlockSpec(memory_space=pl.ANY)
-    vmem = pl.BlockSpec(memory_space=pltpu.VMEM)
     shape = jax.ShapeDtypeStruct
     args = (
         inputs, ln1_gain, ln1_shift, w_qkv, q_bias, v_bias, w_out, out_bias, table_x.T, table_y.T, ln2_gain, ln2_shift,
         w_up, up_bias, w_down, down_bias, cotangent, page_ids, corners,
     )
-    large = (3, 6, 12, 14)
     output, grad_inputs, full_up, full_down, full_qkv, full_out, small = pl.pallas_call(
         functools.partial(layer_kernel, outer),
         out_shape=(
@@ -560,9 +593,12 @@
             shape(w_up.shape, BF16), shape(w_down.shape, BF16), shape(w_qkv.shape, BF16), shape(w_out.shape, BF16),
             shape((SMALL_ROWS, WIDTH), F32),
         ),
-        in_specs=[hbm if k in large else vmem for k in range(len(args))],
-        out_specs=(hbm,) * 6 + (vmem,),
-        scratch_shapes=[
+        in_specs=[hbm] * len(args),
+        out_specs=(hbm,) * 7,
+        scratch_shapes=[pltpu.VMEM((WIDTH,), F32)] * 8
+        + [
+            pltpu.VMEM((FF,), F32), pltpu.VMEM((HEADS, BUCKETS), F32), pltpu.VMEM((HEADS, BUCKETS), F32),
+            pltpu.VMEM(page_ids.shape, jnp.int32), pltpu.VMEM(corners.shape, jnp.int32), pltpu.VMEM((SMALL_ROWS, WIDTH), F32),
             pltpu.VMEM(w_qkv.shape, BF16), pltpu.VMEM(w_out.shape, BF16),
             pltpu.VMEM(w_up.shape, BF16), pltpu.VMEM(w_down.shape, BF16),
             pltpu.VMEM((SQUARES, SIDE, SIDE), BF16),
@@ -579,12 +615,11 @@
             pltpu.VMEM((2, OWN, WIDTH), BF16), pltpu.VMEM((2, OWN, WIDTH), BF16),
             pltpu.VMEM((OWN, WIDTH), BF16), pltpu.VMEM((FULL, 384), BF16), pltpu.VMEM((OWN, WIDTH), BF16),
             pltpu.VMEM((OWN, 3 * WIDTH), BF16), pltpu.VMEM((FULL, 1152), BF16),
-            pltpu.VMEM((OWN, FULL), jnp.int32), pltpu.VMEM((OWN, FULL), jnp.int32),
-            pltpu.VMEM((3, FULL, 128), jnp.int32),
-            pltpu.VMEM((FULL, 128), BF16), pltpu.VMEM((128, OWN), BF16), pltpu.VMEM((HEADS, 128), F32),
+            pltpu.VMEM((3, FULL, 128), jnp.int32), pltpu.VMEM((FULL, 256), BF16),
+            pltpu.VMEM((FULL, 128), BF16), pltpu.VMEM((128, OWN), BF16), pltpu.VMEM((9, 16, 128), F32),
             pltpu.VMEM((BLOCK, WIDTH), BF16), pltpu.VMEM((BLOCK, WIDTH), BF16),
             pltpu.VMEM((BLOCK, WIDTH), BF16), pltpu.VMEM((BLOCK, WIDTH), BF16),
-            pltpu.SemaphoreType.DMA((6,)),
+            pltpu.SemaphoreType.DMA((22,)),
             pltpu.SemaphoreType.DMA((32, 2)),
             pltpu.SemaphoreType.DMA((CHUNKS, slots, 2)),
             pltpu.SemaphoreType.DMA((5 + len(outer), 2)),
@@ -604,40 +639,76 @@
 
 
 def finish_kernel(*refs):
-    small, outs = refs[6], refs[7:]
-    for source, target in zip(refs[:6], outs[:6]):
-        target[...] = source[...].astype(target.dtype)
-
-    @pl.when(pl.program_id(0) == 0)
-    def _():
-        outs[6][...] = small[12:SMALL_ROWS, 0:BUCKETS]
-        outs[7][...] = small[12:SMALL_ROWS, BUCKETS : 2 * BUCKETS]
-        for part in range(FF // WIDTH):
-            outs[8][part * WIDTH : (part + 1) * WIDTH] = small[8 + part, :]
-        for slot in range(8):
-            outs[9 + slot][...] = small[slot, :]
+    sources, passed, small_from = refs[:4], refs[4:6], refs[6]
+    targets, kept, little = refs[7:11], refs[11:13], refs[13:24]
+    rings_in, rings_out, outs = refs[24:27], refs[27:30], refs[30:41]
+    held, small, sems_in, sems_out, sems_kept = refs[41:]
+    small_copy = pltpu.make_async_copy(small_from, small, sems_kept.at[4])
+    arrive = [pltpu.make_async_copy(passed[k], held.at[k], sems_kept.at[k]) for k in range(2)]
+    leave = [pltpu.make_async_copy(held.at[k], kept[k], sems_kept.at[2 + k]) for k in range(2)]
+    leave += [pltpu.make_async_copy(outs[k], little[k], sems_kept.at[5 + k]) for k in range(len(outs))]
+    ring_of = (0, 1, 2, 1)
+    pieces = []
+    for k, source in enumerate(sources):
+        tall = SLAB // source.shape[1]
+        pieces += [(k, ring_of[k], pl.ds(first, tall)) for first in range(0, source.shape[0], tall)]
+
+    def fetch(n):
+        k, ring, part = pieces[n]
+        return pltpu.make_async_copy(sources[k].at[part, :], rings_in[ring].at[n % SLOTS], sems_in.at[n])
+
+    def store(n):
+        k, ring, part = pieces[n]
+        return pltpu.make_async_copy(rings_out[ring].at[n % SLOTS], targets[k].at[part, :], sems_out.at[n])
+
+    small_copy.start()
+    for n in range(SLOTS):
+        fetch(n).start()
+    for copy in arrive:
+        copy.start()
+    small_copy.wait()
+    outs[0][...] = small[12:SMALL_ROWS, 0:BUCKETS]
+    outs[1][...] = small[12:SMALL_ROWS, BUCKETS : 2 * BUCKETS]
+    for part in range(FF // WIDTH):
+        outs[2][part * WIDTH : (part + 1) * WIDTH] = small[8 + part, :]
+    for slot in range(8):
+        outs[3 + slot][...] = small[slot, :]
+    for copy in leave[2:]:
+        copy.start()
+    for n in range(len(pieces)):
+        if n == SLOTS:
+            for k in range(2):
+                arrive[k].wait()
+                leave[k].start()
+        fetch(n).wait()
+        if n >= SLOTS:
+            store(n - SLOTS).wait()
+        ring = pieces[n][1]
+        rings_out[ring][n % SLOTS] = rings_in[ring][n % SLOTS].astype(F32)
+        store(n).start()
+        if n + SLOTS < len(pieces):
+            fetch(n + SLOTS).start()
+    for n in range(len(pieces) - SLOTS, len(pieces)):
+        store(n).wait()
+    for copy in leave:
+        copy.wait()
 
 
 def finish(*arrays):
-    steps = 16
-
-    def slab(array):
-        if array.ndim == 3:
-            return pl.BlockSpec((array.shape[0], array.shape[1] // steps, array.shape[2]), lambda i: (0, i, 0))
-        return pl.BlockSpec((array.shape[0] // steps, array.shape[1]), lambda i: (i, 0))
-
-    def whole(shape):
-        return pl.BlockSpec(shape, lambda i: (0,) * len(shape))
-
+    hbm = pl.BlockSpec(memory_space=pl.ANY)
     little = [(HEADS, BUCKETS)] * 2 + [(FF,)] + [(WIDTH,)] * 8
-    slabs = [slab(array) for array in arrays[:6]]
+    widths = [array.shape[1] for array in arrays[:3]]
+    count = sum(array.size for array in arrays[:4]) // SLAB
     return pl.pallas_call(
         finish_kernel,
-        grid=(steps,),
         out_shape=[jax.ShapeDtypeStruct(array.shape, F32) for array in arrays[:6]]
         + [jax.ShapeDtypeStruct(shape, F32) for shape in little],
-        in_specs=slabs + [whole((SMALL_ROWS, WIDTH))],
-        out_specs=slabs + [whole(shape) for shape in little],
+        in_specs=[hbm] * 7,
+        out_specs=[hbm] * (6 + len(little)),
+        scratch_shapes=[pltpu.VMEM((SLOTS, SLAB // width, width), kind) for kind in (BF16, F32) for width in widths]
+        + [pltpu.VMEM(shape, F32) for shape in little]
+        + [pltpu.VMEM((2,) + arrays[4].shape, F32), pltpu.VMEM((SMALL_ROWS, WIDTH), F32)]
+        + [pltpu.SemaphoreType.DMA((size,)) for size in (count, count, 5 + len(little))],
         compiler_params=pltpu.CompilerParams(vmem_limit_bytes=60 * MIB),
         cost_estimate=pl.CostEstimate(flops=10**7, bytes_accessed=45 * 10**6, transcendentals=0),
     )(*arrays)

time: 177 us -> 158 us (0.89)
  Pallas kernels: 176 us -> 157 us
    pallas_call x1, Pallas kernels: 158 us -> 142 us  [per_device(): pl.pallas_call(functools.partial(layer_kernel, outer), out_shape=(shape(i...]
    pallas_call x1, Pallas kernels: 17.6 us -> 15.1 us  [finish(): pl.pallas_call(finish_kernel, out_shape=[jax.ShapeDtypeStruct(array.shape...]
where the time goes in v2:
time: 158 us
  Pallas kernels  157 us (99%)
    pallas_call x1, Pallas kernels, per_device(): pl.pallas_call(functools.partial(layer_kernel, outer), out_shape=(shape(i...  142 us
    pallas_call x1, Pallas kernels, finish(): pl.pallas_call(finish_kernel, out_shape=[jax.ShapeDtypeStruct(array.shape...  15.1 us

profile of v2, /device:TPU:0, one launch (start us, length us, event | category | flops | bytes accessed | tf_op | source)
XLA Modules:
  0.0 157.6 jit_solution(655874601993564342)
XLA Ops:
  0.7 141.7 %shard_map.314 = (f32[2,128,768]{2,1,0:T(8,128)}, f32[2,128,768]{2,1,0:T(8,128)}, bf16[768,3072]{1,0:T(8,128)(2,1)}, bf16[3072,768]{1,0:T(8,128)(2,1)}, bf16[768...) custom-call(bf16[2,128,768]{2,1,0:T(8,128)(2,1)} %x_in.1, f32[768]{0:T(1024)} %ln1_gain_in.1, ...), custom_call_target="tpu_custom_call" | custom-call | flops 12999999488 | bytes 30000000 | tf_op jit(solution)/shard_map/pallas_call | solution.py:589
  142.3 15.1 %shard_map.315 = (f32[768,3072]{1,0:T(8,128)}, f32[3072,768]{1,0:T(8,128)}, f32[768,2304]{1,0:T(8,128)}, f32[768,768]{1,0:T(8,128)}, f32[2,128,768]{2,1,0:T(8,12...) custom-call(bf16[768,3072]{1,0:T(8,128)(2,1)} %get-tuple-element.41., ...), custom_call_target="tpu_custom_call" | custom-call | flops 10000000 | bytes 45000000 | tf_op jit(solution)/shard_map/pallas_call | solution.py:702

commit v3 on v2

--- a/solution.py
+++ b/solution.py
@@ -34,13 +34,14 @@
 ALONG_Y, ALONG_X, NEAR_Z, FAR_Z = ("blk", 2), ("wide", 1), ("wide", 2), ("wide", 4)
 STEPS = {"Y": ALONG_Y, "X": ALONG_X, "1": NEAR_Z, "2": FAR_Z}
 NAMES = "abcdefghijkl"
-ROUTES = ("XY21", "YX12", "1X2Y", "YX12", "XY12", "YX12", "YX12", "1YX2", "XY12", "XY21", "YX12", "12YX")
+ROUTES = ("XY21", "12YX", "YX21", "12YX", "YX12", "XY21", "X12Y", "YX12", "XY21", "XY12", "YX12", "YX12")
 PLAN = (
-    ("ab",), ("cd",), ("",), ("",), ("ef",), ("h",), ("abc",), ("lde",), ("hb",), ("fc",), ("gld",), ("b",),
-    ("fac",), ("ed",), ("ijhl",), ("kbf",),
-    ("segacsdlbifaedbkajfhedcgsflaheibgjckhiadgsekjfil", "gsjcbkhigbjsdadacfkicelfkejghikljhhigilgljkjk"),
+    ("ab",), ("cd",), ("",), ("",), ("ef",), ("ghab",), ("c",), ("dfe",), ("",), ("lbgh",), ("ca",), ("deg",),
+    ("h",), ("cfea",), ("ijhgc",), ("kl",),
+    ("sbfdasgechfaiekcfjhseglabdhifkljgcskailjefbdgshi", "kclcjias"),
+    ("aklebejdfkifjhghbgiljkdblbilidkdjkj",),
 )
-SMALL_ROWS = 24
+SMALL_ROWS = 16
 
 SLAB = 384 * WIDTH
 SLOTS = 8
@@ -142,19 +143,25 @@
         box += size
     kept = pltpu.make_async_copy(mine.at[rows(first, size), :], place(first, size), sems.at[next(free), 0])
     kept.start()
+    copies = []
     for step, before in zip(reversed(route), reversed(firsts)):
         source = mine.at[rows(first, size), :] if size == PIECE else place(first, size)
-        copy = remote(source, place(first, size), sems.at[next(free)], step)
-        copy.start()
+        copies.append(remote(source, place(first, size), sems.at[next(free)], step))
+        if size == SIDE // 2:
+            copies.append(remote(source, source, sems.at[next(free)], SIBLING))
+        for copy in copies:
+            copy.start()
         yield
-        copy.wait()
+        copies.pop(0).wait()
         if size == PIECE:
             kept.wait()
-        first, size = before, size * 2
-    copy = remote(place(0, SIDE), place(0, SIDE), sems.at[next(free)], SIBLING)
-    copy.start()
+        first, size, arrived = before, size * 2, before + size - (first - before)
+    late = place(arrived, SIDE // 2)
+    copies.append(remote(late, late, sems.at[next(free)], SIBLING))
+    copies[1].start()
     yield
-    copy.wait()
+    for copy in copies:
+        copy.wait()
 
 
 def small_task(steps, total, inbox, sems):
@@ -227,9 +234,7 @@
 
     for copy in loads:
         copy.start()
-    pl.semaphore_wait(pltpu.get_barrier_semaphore(), len(inner + outer))
-    x_copy = exchange(x_in.at[other], x_all.at[pl.ds(BLOCK, BLOCK), :], ALONG_Y)
-    g_copy = exchange(cot_in.at[other], g_all.at[pl.ds(BLOCK, BLOCK), :], ALONG_Y)
+    small[...] = jnp.zeros_like(small)
     loaded(4)
 
     def along(kind, block):
@@ -258,6 +263,8 @@
     def own_lanes(kind, part, mask):
         return jnp.concatenate([jnp.bitwise_and(col[kind, part, :], mask)] * 4, axis=1)
 
+    pl.semaphore_wait(pltpu.get_barrier_semaphore(), len(inner + outer))
+    x_copy = exchange(x_in.at[other], x_all.at[pl.ds(BLOCK, BLOCK), :], ALONG_Y)
 
     at = lax.broadcasted_iota(jnp.int32, (16, 128), 1)
     at = jnp.where(at < BUCKETS, jnp.minimum(at, BUCKETS // 2 - 1), jnp.maximum(at - 128, -(BUCKETS // 2))) + BUCKETS // 2
@@ -311,16 +318,17 @@
             shared.append(exchange(held.at[part, :], held.at[pl.ds(OWN + part.start, BLOCK), :], SIBLING))
 
     first_norm(quarters[0])
-    lax.fori_loop(0, 4, bias_pair, 0)
+    lax.fori_loop(0, PAIRS - 1, bias_pair, 0)
 
     loaded(8)
     gain2, shift2 = ln2_gain[...].reshape(1, WIDTH), ln2_shift[...].reshape(1, WIDTH)
     x_copy.wait()
+    g_copy = exchange(cot_in.at[other], g_all.at[pl.ds(BLOCK, BLOCK), :], ALONG_Y)
     first_norm(quarters[1])
     xn1_copy = exchange(xn1.at[pl.ds(0, OWN), :], xn1.at[pl.ds(OWN, OWN), :], SIBLING)
     joined = (dot(xn1[0:OWN, :], w_qkv[:, 0:WIDTH]) + q_bias[...].reshape(1, WIDTH)).astype(BF16)
     query[...] = joined * jnp.asarray(HEAD_DIM**-0.5, BF16)
-    lax.fori_loop(4, PAIRS, bias_pair, 0)
+    bias_pair(PAIRS - 1, 0)
     for copy in shared:
         copy.wait()
 
@@ -331,19 +339,17 @@
     def join_heads(stacked):
         return jnp.where(low_lane, stacked[0:OWN], stacked[OWN:])
 
-    def attend(pair, carry):
-        here = lanes(pair * 128, 128)
-        q_two = split_heads(query[:, here])
+    for pair in range(PAIRS):
+        here = slice(pair * 128, pair * 128 + 128)
+        q_two, low = split_heads(query[:, here]), (low_a, low_b)[pair % 2]
         for part in quarters:
             masked = dot_cols(q_two[part], keys[:, here]) + probs[pair, part, :]
             terms = jnp.exp(masked - jnp.max(masked, axis=-1, keepdims=True))
             weights = terms * (1.0 / jnp.sum(terms, axis=-1, keepdims=True))
             probs[pair, part, :] = weights
-            low_a[part, :] = weights.astype(BF16)
-        att[0:OWN, here] = join_heads(dot(low_a[...], values[:, here])).astype(BF16)
-        return carry
-
-    lax.fori_loop(0, PAIRS, attend, 0)
+            low[part, :] = weights.astype(BF16)
+        att[0:OWN, here] = join_heads(dot(low[...], values[:, here])).astype(BF16)
+
     att_copy = exchange(att.at[pl.ds(0, OWN), :], att.at[pl.ds(OWN, OWN), :], SIBLING)
     g_copy.wait()
     gs_copy = exchange(g_all.at[pl.ds(0, OWN), :], g_all.at[pl.ds(OWN, OWN), :], SIBLING)
@@ -506,8 +512,8 @@
                 inside = pltpu.roll(line_sum, 96, 1)
                 found.append(jnp.where(spot == 0, below, jnp.where(spot == BUCKETS - 1, above, inside)))
             merged = jnp.where(spot < BUCKETS, found[0], pltpu.roll(found[1], BUCKETS, 1))
-            at = 12 + 2 * pair + odd
-            small[at : at + 1, :] = jnp.concatenate((merged, jnp.zeros((1, WIDTH - 128), F32)), axis=1)
+            line, spot_in = table_spot(2 * pair + odd)
+            small[line : line + 1, spot_in : spot_in + 128] = merged
 
     shared = []
     for pair in range(PAIRS):
@@ -556,10 +562,8 @@
     own_in.start()
 
     pump()
-    out_copy.wait()
-    own_out.wait()
-    in_copy.wait()
-    own_in.wait()
+    for copy in (out_copy, own_out, in_copy, own_in):
+        copy.wait()
     total[0:BLOCK, :] = out_far[...].astype(F32)
     middle[0:BLOCK, :] = in_far[...].astype(F32)
     last = (
@@ -569,6 +573,7 @@
     )
     for copy in last:
         copy.start()
+    pump()
     for copy in last:
         copy.wait()
 
@@ -578,7 +583,7 @@
     w_up, up_bias, w_down, down_bias, cotangent, page_ids, corners,
 ):
     outer = outer_steps(lax.axis_size("wide"))
-    slots = 10 + len(outer)
+    slots = 11 + len(outer)
     assert inputs.shape == (2, BLOCK, WIDTH) and lax.axis_size("blk") == 4 and lax.axis_size("wide") >= 8
     hbm = pl.BlockSpec(memory_space=pl.ANY)
     shape = jax.ShapeDtypeStruct
@@ -638,6 +643,10 @@
     )
 
 
+def table_spot(head):
+    return 12 + head * 128 // WIDTH, head * 128 % WIDTH
+
+
 def finish_kernel(*refs):
     sources, passed, small_from = refs[:4], refs[4:6], refs[6]
     targets, kept, little = refs[7:11], refs[11:13], refs[13:24]
@@ -667,8 +676,11 @@
     for copy in arrive:
         copy.start()
     small_copy.wait()
-    outs[0][...] = small[12:SMALL_ROWS, 0:BUCKETS]
-    outs[1][...] = small[12:SMALL_ROWS, BUCKETS : 2 * BUCKETS]
+    for head in range(HEADS):
+        line, first = table_spot(head)
+        for kind in range(2):
+            start = first + kind * BUCKETS
+            outs[kind][head : head + 1, :] = small[line : line + 1, start : start + BUCKETS]
     for part in range(FF // WIDTH):
         outs[2][part * WIDTH : (part + 1) * WIDTH] = small[8 + part, :]
     for slot in range(8):

time: 158 us -> 154 us (0.975)
  Pallas kernels: 157 us -> 153 us
    pallas_call x1, Pallas kernels: 142 us -> 138 us  [per_device(): pl.pallas_call(functools.partial(layer_kernel, outer), out_shape=(shape(i...]
where the time goes in v3:
time: 154 us
  Pallas kernels  153 us (99%)
    pallas_call x1, Pallas kernels, per_device(): pl.pallas_call(functools.partial(layer_kernel, outer), out_shape=(shape(i...  138 us
    pallas_call x1, Pallas kernels, finish(): pl.pallas_call(finish_kernel, out_shape=[jax.ShapeDtypeStruct(array.shape...  15.1 us

profile of v3, /device:TPU:0, one launch (start us, length us, event | category | flops | bytes accessed | tf_op | source)
XLA Modules:
  0.0 153.6 jit_solution(6543419771034317023)
XLA Ops:
  0.7 137.6 %shard_map.314 = (f32[2,128,768]{2,1,0:T(8,128)}, f32[2,128,768]{2,1,0:T(8,128)}, bf16[768,3072]{1,0:T(8,128)(2,1)}, bf16[3072,768]{1,0:T(8,128)(2,1)}, bf16[768...) custom-call(bf16[2,128,768]{2,1,0:T(8,128)(2,1)} %x_in.1, f32[768]{0:T(1024)} %ln1_gain_in.1, ...), custom_call_target="tpu_custom_call" | custom-call | flops 12999999488 | bytes 30000000 | tf_op jit(solution)/shard_map/pallas_call | solution.py:594
  138.3 15.1 %shard_map.315 = (f32[768,3072]{1,0:T(8,128)}, f32[3072,768]{1,0:T(8,128)}, f32[768,2304]{1,0:T(8,128)}, f32[768,768]{1,0:T(8,128)}, f32[2,128,768]{2,1,0:T(8,12...) custom-call(bf16[768,3072]{1,0:T(8,128)(2,1)} %get-tuple-element.41., ...), custom_call_target="tpu_custom_call" | custom-call | flops 10000000 | bytes 45000000 | tf_op jit(solution)/shard_map/pallas_call | solution.py:714

commit v4 on v3

--- a/solution.py
+++ b/solution.py
@@ -34,12 +34,13 @@
 ALONG_Y, ALONG_X, NEAR_Z, FAR_Z = ("blk", 2), ("wide", 1), ("wide", 2), ("wide", 4)
 STEPS = {"Y": ALONG_Y, "X": ALONG_X, "1": NEAR_Z, "2": FAR_Z}
 NAMES = "abcdefghijkl"
-ROUTES = ("XY21", "12YX", "YX21", "12YX", "YX12", "XY21", "X12Y", "YX12", "XY21", "XY12", "YX12", "YX12")
+ROUTES = ("XY12", "Y1X2", "XY12", "YX12", "1XY2", "XY12", "X1Y2", "21YX", "Y1X2", "XY21", "XY12", "YX12")
 PLAN = (
-    ("ab",), ("cd",), ("",), ("",), ("ef",), ("ghab",), ("c",), ("dfe",), ("",), ("lbgh",), ("ca",), ("deg",),
-    ("h",), ("cfea",), ("ijhgc",), ("kl",),
-    ("sbfdasgechfaiekcfjhseglabdhifkljgcskailjefbdgshi", "kclcjias"),
-    ("aklebejdfkifjhghbgiljkdblbilidkdjkj",),
+    ("ba",), ("",), ("",), ("",), ("ecd",), ("agfh",), ("b",), ("",), ("",), ("cdlag",),
+    ("",), ("ca",), ("hfbecd",), ("blgaf",), ("ejhcblif",), ("cklbechjdfalicgklaj",),
+    ("figkhdlfjasebihjkgsldcfgdekshgbikjslkhi",),
+    ("ejafdkgbifcesijklehadghs",),
+    ("ijdebkij",),
 )
 SMALL_ROWS = 16
 
@@ -571,8 +572,10 @@
         pltpu.make_async_copy(middle.at[pl.ds(0, BLOCK), :], o_inputs.at[other], load_sems.at[20]),
         pltpu.make_async_copy(small, o_small, load_sems.at[21]),
     )
-    for copy in last:
+    for copy in last[:2]:
         copy.start()
+    pump()
+    last[2].start()
     pump()
     for copy in last:
         copy.wait()

time: 154 us -> 153 us (level)
  Pallas kernels: 153 us -> 151 us
where the time goes in v4:
time: 153 us; the launch traced here: 152 us
  Pallas kernels  151 us (99%)
    pallas_call x1, Pallas kernels, per_device(): pl.pallas_call(functools.partial(layer_kernel, outer), out_shape=(shape(i...  136 us
    pallas_call x1, Pallas kernels, finish(): pl.pallas_call(finish_kernel, out_shape=[jax.ShapeDtypeStruct(array.shape...  15.1 us

profile of v4, /device:TPU:0, one launch (start us, length us, event | category | flops | bytes accessed | tf_op | source)
XLA Modules:
  0.0 152.3 jit_solution(9225275743191329713)
XLA Ops:
  0.7 136.4 %shard_map.314 = (f32[2,128,768]{2,1,0:T(8,128)}, f32[2,128,768]{2,1,0:T(8,128)}, bf16[768,3072]{1,0:T(8,128)(2,1)}, bf16[3072,768]{1,0:T(8,128)(2,1)}, bf16[768...) custom-call(bf16[2,128,768]{2,1,0:T(8,128)(2,1)} %x_in.1, f32[768]{0:T(1024)} %ln1_gain_in.1, ...), custom_call_target="tpu_custom_call" | custom-call | flops 12999999488 | bytes 30000000 | tf_op jit(solution)/shard_map/pallas_call | solution.py:597
  137.1 15.1 %shard_map.315 = (f32[768,3072]{1,0:T(8,128)}, f32[3072,768]{1,0:T(8,128)}, f32[768,2304]{1,0:T(8,128)}, f32[768,768]{1,0:T(8,128)}, f32[2,128,768]{2,1,0:T(8,12...) custom-call(bf16[768,3072]{1,0:T(8,128)(2,1)} %get-tuple-element.41., ...), custom_call_target="tpu_custom_call" | custom-call | flops 10000000 | bytes 45000000 | tf_op jit(solution)/shard_map/pallas_call | solution.py:717

commit v5 on v4

--- a/solution.py
+++ b/solution.py
@@ -34,18 +34,18 @@
 ALONG_Y, ALONG_X, NEAR_Z, FAR_Z = ("blk", 2), ("wide", 1), ("wide", 2), ("wide", 4)
 STEPS = {"Y": ALONG_Y, "X": ALONG_X, "1": NEAR_Z, "2": FAR_Z}
 NAMES = "abcdefghijkl"
-ROUTES = ("XY12", "Y1X2", "XY12", "YX12", "1XY2", "XY12", "X1Y2", "21YX", "Y1X2", "XY21", "XY12", "YX12")
+ROUTES = ("YX21", "XY12", "XY12", "Y1X2", "2YX1", "XY12", "XY12", "12XY", "Y1X2", "XY12", "XY12", "YX12")
 PLAN = (
-    ("ba",), ("",), ("",), ("",), ("ecd",), ("agfh",), ("b",), ("",), ("",), ("cdlag",),
-    ("",), ("ca",), ("hfbecd",), ("blgaf",), ("ejhcblif",), ("cklbechjdfalicgklaj",),
-    ("figkhdlfjasebihjkgsldcfgdekshgbikjslkhi",),
-    ("ejafdkgbifcesijklehadghs",),
-    ("ijdebkij",),
+    ("ab",), ("",), ("",), ("d",), ("ce",), ("ahb",), ("",), ("lgf",), ("acb",), ("hd",),
+    ("bega",), ("",), ("dfcl",), ("ecabh",), ("jil",), ("ceaf",),
+    ("cklgadcbfhjdelchbigksejafldsgibjkilgkfeghijfdksa", "c"),
+    ("igjhlckafjibksdehjlkisbjfgdjghelkidefs",),
+    ("khi",),
 )
 SMALL_ROWS = 16
 
 SLAB = 384 * WIDTH
-SLOTS = 8
+SLOTS = 10
 
 
 def outer_steps(wide):

time: 153 us -> 150 us (0.980)
  Pallas kernels: 151 us -> 149 us
    pallas_call x1, Pallas kernels: 136 us -> 134 us  [per_device(): pl.pallas_call(functools.partial(layer_kernel, outer), out_shape=(shape(i...]
where the time goes in v5:
time: 150 us
  Pallas kernels  149 us (99%)
    pallas_call x1, Pallas kernels, per_device(): pl.pallas_call(functools.partial(layer_kernel, outer), out_shape=(shape(i...  134 us
    pallas_call x1, Pallas kernels, finish(): pl.pallas_call(finish_kernel, out_shape=[jax.ShapeDtypeStruct(array.shape...  14.9 us

profile of v5, /device:TPU:0, one launch (start us, length us, event | category | flops | bytes accessed | tf_op | source)
XLA Modules:
  0.0 150.0 jit_solution(17861900174524399153)
XLA Ops:
  0.7 134.2 %shard_map.314 = (f32[2,128,768]{2,1,0:T(8,128)}, f32[2,128,768]{2,1,0:T(8,128)}, bf16[768,3072]{1,0:T(8,128)(2,1)}, bf16[3072,768]{1,0:T(8,128)(2,1)}, bf16[768...) custom-call(bf16[2,128,768]{2,1,0:T(8,128)(2,1)} %x_in.1, f32[768]{0:T(1024)} %ln1_gain_in.1, ...), custom_call_target="tpu_custom_call" | custom-call | flops 12999999488 | bytes 30000000 | tf_op jit(solution)/shard_map/pallas_call | solution.py:597
  134.9 14.9 %shard_map.315 = (f32[768,3072]{1,0:T(8,128)}, f32[3072,768]{1,0:T(8,128)}, f32[768,2304]{1,0:T(8,128)}, f32[768,768]{1,0:T(8,128)}, f32[2,128,768]{2,1,0:T(8,12...) custom-call(bf16[768,3072]{1,0:T(8,128)(2,1)} %get-tuple-element.41., ...), custom_call_target="tpu_custom_call" | custom-call | flops 10000000 | bytes 45000000 | tf_op jit(solution)/shard_map/pallas_call | solution.py:717
